TPU v7x, 32 devices: a whole 2x2x4 slice. The times are simulated.
32 devices in a mesh: dp: 8 (over z, y), tensor: 4 (over x, core).
Axes of the slice: x: 2, y: 2, z: 4, core: 2. Of those that a mesh axis runs over, the one named last changes fastest.
Arguments:
- inputs: bfloat16 [64, 197, 512], P('dp'), may hold values from -24 to 24
- valid_mask: int32 [64, 197], P('dp'), may hold values from 0 to 1
- expert_ids: int32 [64, 197, 2], P('dp'), may hold values from 0 to 31, as said below
- slot_ids: int32 [64, 197, 2], P('dp'), may hold values from 0 to 104, as said below
- norm1_gain: bfloat16 [512], replicated, may hold values from 0.5 to 1.5
- norm1_bias: bfloat16 [512], replicated, may hold values from -3 to 3
- w_qkv: bfloat16 [512, 3, 512], P(None, None, 'tensor'), may hold values from -2 to 2
- b_qv: bfloat16 [2, 512], P(None, 'tensor'), may hold values from -3 to 3
- w_out: bfloat16 [512, 512], P('tensor'), may hold values from -1.5 to 1.5
- b_out: bfloat16 [512], replicated, may hold values from -3 to 3
- norm2_gain: bfloat16 [512], replicated, may hold values from 0.5 to 1.5
- norm2_bias: bfloat16 [512], replicated, may hold values from -3 to 3
- w_router: bfloat16 [512, 32], replicated, may hold values from -0.1875 to 0.1875
- w_in: bfloat16 [32, 512, 2048], P('dp', None, 'tensor'), may hold values from -2 to 2
- b_in: bfloat16 [32, 2048], P('dp', 'tensor'), may hold values from -1.5 to 1.5
- w_back: bfloat16 [32, 2048, 512], P('dp', 'tensor'), may hold values from -0.25 to 0.25
- b_back: bfloat16 [32, 512], replicated, may hold values from -1.5 to 1.5
- cotangent: bfloat16 [64, 197, 512], P('dp'), may hold values from -24 to 24
Outputs:
- output: float32 [64, 197, 512], P('dp')
- d_inputs: float32 [64, 197, 512], P('dp')
- g_norm1_gain: float32 [512], replicated
- g_norm1_bias: float32 [512], replicated
- g_w_qkv: float32 [512, 3, 512], P(None, None, 'tensor')
- g_b_qv: float32 [2, 512], P(None, 'tensor')
- g_w_out: float32 [512, 512], P('tensor')
- g_b_out: float32 [512], replicated
- g_norm2_gain: float32 [512], replicated
- g_norm2_bias: float32 [512], replicated
- g_w_router: float32 [512, 32], replicated
- g_w_in: float32 [32, 512, 2048], P('dp', None, 'tensor')
- g_b_in: float32 [32, 2048], P('dp', 'tensor')
- g_w_back: float32 [32, 2048, 512], P('dp', 'tensor')
- g_b_back: float32 [32, 512], replicated
- grad_norms: float32 [13], replicated
- rms_values: float32 [5], replicated
Inputs may be any that keep to these rules, and one draw needn't show every extreme that they name: `expert_ids`: the two experts of a token differ. `slot_ids`: among the tokens of one block of 8 images, routes to one expert that hold a row below 104 hold different rows; 104 marks a dropped route, and every route of an invalid token is dropped. In every block some expert has all 104 rows used and some route dropped, and one expert has all rows used in every block.
All inputs are finite; a program needn't handle non-finite values.
Results may differ from a plain program's by a relative error of at most 0.025.
Values may be sent and summed in bfloat16 or wider, within the bound.
No kernel may reach another device: no remote copies, remote signals or barrier semaphores. Data moves between devices by JAX's collectives and lax.ppermute only.
A program may use at most 192 MiB of HBM per device.

v0:
```python
import functools

import jax
import jax.numpy as jnp
from jax import lax
from jax.experimental import pallas as pl
from jax.experimental.pallas import tpu as pltpu
from jax.sharding import PartitionSpec as P

D = 512
HD = 64
EXPERTS = 32
SEQ = 197
CAP = 104
PAD = 208
UPS = CAP + 8
WIDE = 256
MIB_HEADS = 58
MIB_EXPERT = 58
MIB_GRADS = 58
MIB_PULL = 58
LANES = 128
F32 = jnp.float32
BF16 = jnp.bfloat16


def nn(a, b):
    return lax.dot_general(a, b, (((1,), (0,)), ((), ())), preferred_element_type=F32)


def nt(a, b):
    return lax.dot_general(a, b, (((1,), (1,)), ((), ())), preferred_element_type=F32)


def tn(a, b):
    return lax.dot_general(a, b, (((0,), (0,)), ((), ())), preferred_element_type=F32)


def swap(value, axis, size, by):
    return lax.ppermute(value, axis, [(at, at ^ by) for at in range(size)])


def after(value, *others):
    return lax.optimization_barrier((value, *others))[0]


class Held:
    def __init__(self, ref, copy):
        self.ref, self.copy, self.there = ref, copy, False
        self.shape, self.dtype = ref.shape, ref.dtype

    def __getitem__(self, index):
        if not self.there:
            self.copy.wait()
            self.there = True
        return self.ref[index]


class Sent:
    def __init__(self, ref, copy):
        self.ref, self.copy, self.left = ref, copy, False
        self.shape, self.dtype = ref.shape, ref.dtype

    def __getitem__(self, index):
        return self.ref[index]

    def __setitem__(self, index, value):
        self.ref[index] = value

    def send(self):
        if not self.left:
            self.copy.start()
            self.left = True


def streamed(kernel, ins, outs, scratch):
    shapes = [(a.shape, a.dtype) for a in ins] + list(outs)

    def body(s_ref, *refs):
        far, refs = refs[: len(shapes)], refs[len(shapes) :]
        near, refs, sems = refs[: len(shapes)], refs[len(shapes) : -1], refs[-1]
        held = []
        for i in range(len(ins)):
            copy = pltpu.make_async_copy(far[i], near[i], sems.at[i])
            copy.start()
            held.append(Held(near[i], copy))
        sent = [
            Sent(near[i], pltpu.make_async_copy(near[i], far[i], sems.at[i]))
            for i in range(len(ins), len(shapes))
        ]
        kernel(s_ref, *held, *sent, *refs)
        for value in held:
            if not value.there:
                value.copy.wait()
        for value in sent:
            value.send()
        for value in sent:
            value.copy.wait()

    buffers = [pltpu.VMEM(shape, dtype) for shape, dtype in shapes]
    return body, [*buffers, *scratch, pltpu.SemaphoreType.DMA((len(shapes),))]


def run(
    kernel, scalars, ins, outs, scratch=(), grid=(1,), in_specs=None, out_specs=None, mib=28, left=(),
    stream=False, aliases=None,
):
    in_specs, out_specs = in_specs or {}, out_specs or {}
    if stream:
        kernel, scratch = streamed(kernel, ins, outs, scratch)
        left = range(len(ins))
        out_specs = {i: pl.BlockSpec(memory_space=pl.ANY) for i in range(len(outs))}

    def whole(shape, stays=False):
        if stays:
            return pl.BlockSpec(memory_space=pl.ANY)
        return pl.BlockSpec(shape, lambda step, s, nd=len(shape): (0,) * nd)

    return pl.pallas_call(
        kernel,
        grid_spec=pltpu.PrefetchScalarGridSpec(
            num_scalar_prefetch=1,
            grid=grid,
            in_specs=[
                in_specs[i] if i in in_specs else whole(a.shape, i in left)
                for i, a in enumerate(ins)
            ],
            out_specs=[out_specs[i] if i in out_specs else whole(o[0]) for i, o in enumerate(outs)],
            scratch_shapes=list(scratch),
        ),
        out_shape=[jax.ShapeDtypeStruct(shape, dtype) for shape, dtype in outs],
        input_output_aliases={i + 1: o for i, o in (aliases or {}).items()},
        compiler_params=pltpu.CompilerParams(vmem_limit_bytes=mib * 2**20),
        cost_estimate=pl.CostEstimate(flops=0, bytes_accessed=0, transcendentals=0),
    )(scalars, *ins)


def route_rows(ids_ref, slots_ref, image):
    ids, slots = ids_ref[image], slots_ref[image]
    return jnp.where(slots < CAP, ids * CAP + slots, -1)


def block_start(s_ref, chunk):
    return (chunk * s_ref[4] + s_ref[5]) * CAP


def target_column(s_ref, chunks):
    rows = lax.broadcasted_iota(jnp.int32, (CAP, 1), 0)
    starts = [block_start(s_ref, chunk) for chunk in range(chunks)]
    return jnp.concatenate([rows + start for start in starts], axis=0)


def target_row(s_ref, chunks):
    lanes = lax.broadcasted_iota(jnp.int32, (1, chunks * CAP), 1)
    target = lanes
    for chunk in range(chunks):
        here = (lanes >= chunk * CAP) & (lanes < (chunk + 1) * CAP)
        target = jnp.where(here, lanes + (block_start(s_ref, chunk) - chunk * CAP), target)
    return target


def spread(source_ref, wide_ref, count):
    for k in range(D // LANES):
        wide_ref[k] = source_ref[:, k * LANES : (k + 1) * LANES].astype(F32)

    def image_rows(image):
        return jnp.concatenate(
            [wide_ref[k, pl.ds(image, SEQ, stride=count), :] for k in range(D // LANES)], axis=1
        )

    return image_rows


def own_rows(images, me, image_rows, out_ref, padded):
    padded[...] = jnp.zeros_like(padded)
    for image in range(images):
        padded[image * PAD : image * PAD + SEQ, :] = image_rows(me * images + image)
    out_ref[...] = padded[...].astype(BF16)


def pack_kernel(width, s_ref, qkv_ref, out_ref, bias_ref, in_bias_ref, pack):
    pack[0 : 3 * D, :] = qkv_ref[...]
    for block in range(D // width):
        at = 3 * D + block * width
        pack[at : at + width, :] = out_ref[:, block * width : (block + 1) * width]
    bias = bias_ref[...].astype(F32)
    experts, hidden = in_bias_ref.shape
    lines = in_bias_ref[...].astype(F32)
    lines = [
        lines[e : e + 1, k * width : (k + 1) * width]
        for e in range(experts)
        for k in range(hidden // width)
    ]
    fill = -len(lines) % 16
    if fill:
        lines.append(jnp.zeros((fill, width), F32))
    pack[4 * D :, :] = jnp.concatenate(
        [bias[0:1], bias[1:2], jnp.zeros((14, width), F32), *lines], axis=0
    ).astype(BF16)


def start_kernel(dims, s_ref, ids_ref, slots_ref, cot_ref, *refs):
    count, images, chunks, shared = dims
    copies = []
    if shared:
        w_in, w_back, *refs = refs
    own, *refs = refs
    near_outs, far_out, refs = refs[: chunks // 2], refs[chunks // 2], refs[chunks // 2 + 1 :]
    if shared:
        *laid, refs = *refs[:3], refs[3:]
    wide, padded, blocks, marks, square, wholes, sems = refs
    if shared:
        hidden = w_back.shape[1]
        for r, target in enumerate(laid, 1):
            expert = jnp.bitwise_xor(s_ref[0], r)
            for side, (source, place) in enumerate(
                ((w_in, pl.ds(0, D)), (w_back, pl.ds(D, hidden)))
            ):
                copies.append(
                    pltpu.make_async_copy(
                        source.at[expert], target.at[place], sems.at[2 * r - 2 + side]
                    )
                )
    for copy in copies:
        copy.start()
    image_rows = spread(cot_ref, wide, count)
    target = target_column(s_ref, chunks)
    rows = chunks * CAP
    blocks[...] = jnp.zeros_like(blocks)
    marks[...] = jnp.zeros_like(marks)

    def step(pair, carry):
        total = jnp.zeros((rows, D), F32)
        others = jnp.zeros((rows, SEQ), F32)
        for image in (2 * pair, 2 * pair + 1):
            flat = route_rows(ids_ref, slots_ref, image)
            ids = ids_ref[image].astype(F32)
            first = target == flat[0:1, :]
            second = target == flat[1:2, :]
            hit = (first | second).astype(F32).astype(BF16)
            total += nn(hit, image_rows(image).astype(BF16))
            others += jnp.where(first, ids[1:2, :], 0.0) + jnp.where(second, ids[0:1, :], 0.0)
        blocks[...] += total
        marks[...] += jnp.broadcast_to(jnp.sum(others, axis=1, keepdims=True), marks.shape)
        return carry

    lax.fori_loop(0, count // 2, step, 0)
    square[...] = jnp.zeros_like(square)
    wholes[...] = jnp.zeros_like(wholes)
    for chunk in range(chunks):
        at = pl.multiple_of(jnp.bitwise_xor(s_ref[3], chunk) * CAP, 8)
        place = chunk * UPS
        wholes[place : place + CAP, :] = blocks[pl.ds(at, CAP), :]
        square[0:CAP, :] = marks[pl.ds(at, CAP), :]
        wholes[place + CAP : place + UPS, 0:LANES] = jnp.transpose(square[...])[0:8, :]
    for chunk, near_out in enumerate(near_outs):
        near_out[...] = wholes[chunk * UPS : (chunk + 1) * UPS, :].astype(BF16)
    far_out[...] = wholes[chunks // 2 * UPS :, :].astype(BF16)
    own_rows(images, s_ref[0], image_rows, own, padded)
    for copy in copies:
        copy.wait()


def padded_routes(ids_ref, slots_ref, image, flat_ref):
    flat_ref[...] = jnp.full(flat_ref.shape, -1, jnp.int32)
    flat_ref[0:2, 0:SEQ] = route_rows(ids_ref, slots_ref, image)
    return flat_ref[...]


def dispatch_kernel(groups, images, chunks, s_ref, ids_ref, slots_ref, *refs):
    tokens, (far, late, out, *passed, flat_ref) = refs[:groups], refs[groups:]
    for chunk, on in enumerate(passed, 1):
        on[0:UPS, :] = far[chunk * UPS : (chunk + 1) * UPS, :]
    passed[-1][UPS:, :] = late[...]
    me = s_ref[0]
    target = target_column(s_ref, chunks)
    total = jnp.zeros((chunks * CAP, D), F32)
    for group in range(groups):
        for image in range(images):
            at = jnp.bitwise_xor(me, group) * images + image
            flat = padded_routes(ids_ref, slots_ref, at, flat_ref)[:, :PAD]
            hit = (target == flat[0:1, :]) | (target == flat[1:2, :])
            total += nn(
                hit.astype(F32).astype(BF16), tokens[group][image * PAD : (image + 1) * PAD, :]
            )
    out[...] = total.astype(BF16)


def combine_kernel(groups, images, chunks, s_ref, ids_ref, slots_ref, rows_ref, *refs):
    outs, flat_ref = refs[:2], refs[2]
    me = s_ref[0]
    rows = rows_ref[...]
    target = target_row(s_ref, chunks)

    def step(pair, carry):
        for odd in range(2):
            for image in range(images):
                at = jnp.bitwise_xor(me, 2 * pair + odd) * images + image
                flat = jnp.transpose(padded_routes(ids_ref, slots_ref, at, flat_ref))[:PAD, :]
                hit = (flat[:, 0:1] == target) | (flat[:, 1:2] == target)
                place = pl.multiple_of((pair * images + image) * PAD, 16)
                outs[odd][pl.ds(place, PAD), :] = nn(
                    hit.astype(F32).astype(BF16), rows
                ).astype(BF16)
        return carry

    lax.fori_loop(0, groups // 2, step, 0)


def chunk_weights(packs, width):
    qkv = [p[part * D : (part + 1) * D, :] for p in packs for part in range(3)]
    biases = []
    for p in packs:
        lines = p[3 * D + D : 3 * D + D + 16, :].astype(F32)
        biases += [lines[0:1], jnp.zeros((1, width), F32), lines[1:2]]
    outs = [
        jnp.concatenate(
            [p[3 * D + b * width : 3 * D + (b + 1) * width, :] for b in range(D // width)], axis=1
        )
        for p in packs
    ]
    return (
        jnp.concatenate(qkv, axis=1),
        jnp.concatenate(biases, axis=1),
        jnp.concatenate(outs, axis=0),
    )


def normalize(values):
    average = jnp.mean(values, axis=-1, keepdims=True)
    centered = values - average
    inv_std = lax.rsqrt(jnp.mean(centered * centered, axis=-1, keepdims=True) + 1e-06)
    return centered * inv_std, inv_std


def norm_pull(upstream, normal, inv_std, gain):
    scaled = upstream * gain
    inner = jnp.mean(scaled * normal, axis=-1, keepdims=True)
    return inv_std * (scaled - jnp.mean(scaled, axis=-1, keepdims=True) - normal * inner)


def key_masks(images, me, mask_ref, pad_ref):
    pad_ref[...] = jnp.full(pad_ref.shape, -1, jnp.int32)
    for image in range(images):
        pad_ref[image : image + 1, 0:SEQ] = mask_ref[pl.ds(me * images + image, 1), :]
    return pad_ref[...]


def valid_column(images, masks):
    columns = jnp.transpose(jnp.maximum(masks, 0).astype(F32))
    return jnp.concatenate([columns[:PAD, i : i + 1] for i in range(images)], axis=0)


def probabilities_of(queries, key_rows, key_mask):
    shift = jnp.where(key_mask > 0, 0.0, jnp.where(key_mask < 0, -2e30, -1e30))
    scores = nt(queries * jnp.asarray(HD ** (-0.5), BF16), key_rows) + shift
    exps = jnp.exp(scores - jnp.max(scores, axis=-1, keepdims=True))
    return exps * (1.0 / jnp.sum(exps, axis=-1, keepdims=True))


def by_head(rows, heads):
    zeros = jnp.zeros_like(rows)
    width = rows.shape[1]
    return jnp.concatenate(
        [jnp.where(head_lanes(width, head), rows, zeros) for head in range(heads)], axis=0
    )


def own_lanes(stacked, heads):
    result = stacked[:PAD]
    for head in range(1, heads):
        lanes = head_lanes(stacked.shape[1], head)
        result = jnp.where(lanes, stacked[head * PAD : (head + 1) * PAD], result)
    return result


def head_lanes(width, head):
    lane = lax.broadcasted_iota(jnp.int32, (1, width), 1)
    return (lane >= head * HD) & (lane < (head + 1) * HD)


def attend(images, heads, width, chunks, normed, weight, bias, masks, projected_ref):
    projected = (nn(normed, weight) + bias).astype(BF16)
    projected_ref[...] = projected
    projected_ref.send()
    parts = []
    for image in range(images):
        key_mask = masks[image : image + 1, :PAD]
        line = []
        for chunk in range(chunks):
            queries, key_rows, values = (
                projected[
                    image * PAD : (image + 1) * PAD,
                    (3 * chunk + part) * width : (3 * chunk + part + 1) * width,
                ]
                for part in range(3)
            )
            own = by_head(queries, heads)
            probabilities = probabilities_of(own, key_rows, key_mask)
            mixed = own_lanes(nn(probabilities.astype(BF16), values), heads)
            line.append(mixed.astype(BF16))
        parts.append(jnp.concatenate(line, axis=1))
    return projected, jnp.concatenate(parts, axis=0)


def heads_kernel(count, images, heads, width, chunks, s_ref, x_ref, norms_ref, mask_ref, *refs):
    packs, outs = refs[:chunks], refs[chunks : chunks + 7]
    wide, padded, mask_pad = refs[-3:]
    x_own, normed_ref, normed2_ref, middle_ref, sums, projected_ref, attended_ref = outs
    own_rows(images, s_ref[0], spread(x_ref, wide, count), x_own, padded)
    x_own.send()
    stream = padded[...]
    normal, _ = normalize(stream)
    normed = (normal * norms_ref[0:1, :] + norms_ref[1:2, :]).astype(BF16)
    normed_ref[...] = normed
    normed_ref.send()
    masks = key_masks(images, s_ref[0], mask_ref, mask_pad)
    weight, bias, out_weight = chunk_weights(packs, width)
    projected, attended = attend(
        images, heads, width, chunks, normed, weight, bias, masks, projected_ref
    )
    attended_ref[...] = attended
    attended_ref.send()
    branch = nn(attended, out_weight) + norms_ref[4:5, :]
    middle = stream + branch
    normal, _ = normalize(middle)
    normed2_ref[...] = (normal * norms_ref[2:3, :] + norms_ref[3:4, :]).astype(BF16)
    normed2_ref.send()
    middle_ref[...] = middle.astype(BF16)
    middle_ref.send()
    valid = valid_column(images, masks)
    sums[...] = jnp.concatenate(
        [
            jnp.sum(middle * middle * valid, axis=0, keepdims=True),
            jnp.sum(branch * branch * valid, axis=0, keepdims=True),
            jnp.broadcast_to(jnp.sum(valid, axis=0, keepdims=True), (1, D)),
            jnp.zeros((5, D), F32),
        ],
        axis=0,
    )


def as_lines(rows):
    return jnp.concatenate([rows[:, k * LANES : (k + 1) * LANES] for k in range(D // LANES)], axis=0)


def as_rows(lines):
    count = lines.shape[0] // (D // LANES)
    return jnp.concatenate(
        [lines[k * count : (k + 1) * count] for k in range(D // LANES)], axis=1
    )


def attend_pull(images, heads, width, chunks, projected_ref, d_attended, masks):
    parts = []
    for image in range(images):
        span = slice(image * PAD, (image + 1) * PAD)
        key_mask = masks[image : image + 1, :PAD]
        line = []
        for chunk in range(chunks):
            queries, key_rows, values = (
                projected_ref[span, (3 * chunk + part) * width : (3 * chunk + part + 1) * width]
                for part in range(3)
            )
            d_mixed = d_attended[span, chunk * width : (chunk + 1) * width]
            own = by_head(queries, heads)
            d_own = by_head(d_mixed, heads)
            probabilities = probabilities_of(own, key_rows, key_mask)
            d_probs = nt(d_own, values)
            row_dots = jnp.sum(d_probs * probabilities, axis=-1, keepdims=True)
            d_scores = probabilities * (d_probs - row_dots)
            d_scores = jnp.where(key_mask > 0, d_scores, 0.0).astype(BF16)
            d_values = tn(probabilities.astype(BF16), d_own)
            d_queries = own_lanes(nn(d_scores, key_rows), heads)
            d_keys = tn(d_scores, own)
            line += [d_queries * HD ** (-0.5), d_keys * HD ** (-0.5), d_values]
        parts.append(jnp.concatenate(line, axis=1).astype(BF16))
    return jnp.concatenate(parts, axis=0)


def heads_pull(
    dims, s_ref, normed, projected_ref, attended_ref, d_branch, packs, masks, router_ref, grads, biases
):
    images, heads, width, chunks, start, groups = dims
    weight, _, out_weight = chunk_weights(packs, width)
    d_attended = nt(d_branch, out_weight).astype(BF16)
    d_project = attend_pull(images, heads, width, chunks, projected_ref, d_attended, masks)
    grad = tn(normed, d_project)
    out_grad = tn(attended_ref[...], d_branch)
    for chunk in range(chunks):
        for part in range(3):
            at = (3 * chunk + part) * width
            grads[chunk][part * D : (part + 1) * D, :] = grad[:, at : at + width].astype(BF16)
        for block in range(D // width):
            at = 3 * D + block * width
            grads[chunk][at : at + width, :] = out_grad[
                chunk * width : (chunk + 1) * width, block * width : (block + 1) * width
            ].astype(BF16)
        per = EXPERTS // groups
        owner = jnp.bitwise_xor(s_ref[0], start + chunk)
        router = router_ref[0:per, :]
        for g in range(1, groups):
            router = jnp.where(owner == g, router_ref[g * per : (g + 1) * per, :], router)
        router = as_lines(router)
        grads[chunk][4 * D : 4 * D + router.shape[0], :] = router.astype(BF16)
        rest = grads[chunk].shape[0] - 4 * D - router.shape[0]
        if rest:
            grads[chunk][4 * D + router.shape[0] :, :] = jnp.zeros((rest, width), BF16)
    biases[...] = jnp.broadcast_to(
        jnp.sum(d_project.astype(F32), axis=0, keepdims=True), biases.shape
    )
    return nt(d_project, weight)


def middle_pull_kernel(
    dims, s_ref, cot_ref, part_ref, near_ref, top_ref, rest_ref, middle_ref, norms_ref, normed_ref, mask_ref,
    projected_ref, attended_ref, router_ref, *refs,
):
    images, chunks = dims[0], dims[3]
    packs, outs, mask_pad = refs[:chunks], refs[chunks:-1], refs[-1]
    d_low, sums, d_branch_ref, biases = outs[:4]
    tokens = images * PAD
    normal, inv_std = normalize(middle_ref[...].astype(F32))
    d_normed2 = part_ref[...][:tokens].astype(F32) + near_ref[...][:tokens].astype(F32)
    d_normed2 = d_normed2 + jnp.concatenate([top_ref[...], rest_ref[...]], axis=0).astype(F32)
    d_middle = cot_ref[...].astype(F32) + norm_pull(d_normed2, normal, inv_std, norms_ref[2:3, :])
    d_branch = d_middle.astype(BF16)
    d_branch_ref[...] = d_branch
    sums[...] = jnp.concatenate(
        [
            jnp.sum(d_normed2 * normal, axis=0, keepdims=True),
            jnp.sum(d_normed2, axis=0, keepdims=True),
            jnp.sum(d_branch.astype(F32), axis=0, keepdims=True),
            jnp.zeros((5, D), F32),
        ],
        axis=0,
    )
    masks = key_masks(images, s_ref[0], mask_ref, mask_pad)
    d_low[...] = heads_pull(
        dims, s_ref, normed_ref[...], projected_ref, attended_ref, d_branch, packs, masks, router_ref,
        outs[4:], biases,
    ).astype(BF16)


def input_pull_kernel(
    dims, s_ref, x_ref, d_normed_ref, d_branch_ref, norms_ref, normed_ref, mask_ref,
    projected_ref, attended_ref, router_ref, *refs,
):
    images, chunks = dims[0], dims[3]
    packs, outs, mask_pad = refs[:chunks], refs[chunks:-1], refs[-1]
    d_inputs_ref, sums, biases = outs[:3]
    masks = key_masks(images, s_ref[0], mask_ref, mask_pad)
    d_normed = d_normed_ref[...].astype(F32) + heads_pull(
        dims, s_ref, normed_ref[...], projected_ref, attended_ref, d_branch_ref[...], packs, masks,
        router_ref, outs[3:], biases,
    )
    normal, inv_std = normalize(x_ref[...].astype(F32))
    d_inputs = d_branch_ref[...].astype(F32) + norm_pull(d_normed, normal, inv_std, norms_ref[0:1, :])
    d_inputs_ref[...] = d_inputs.astype(BF16)
    sums[...] = jnp.concatenate(
        [
            jnp.sum(d_normed * normal, axis=0, keepdims=True),
            jnp.sum(d_normed, axis=0, keepdims=True),
            jnp.sum(d_inputs * d_inputs * valid_column(images, masks), axis=0, keepdims=True),
            jnp.zeros((5, D), F32),
        ],
        axis=0,
    )


def expert_kernel(dims, s_ref, rows_in, *refs):
    chunks, pieces, hidden_width, width = dims
    ups_in, refs = refs[: chunks - 1], refs[chunks - 1 :]
    biases, refs = refs[:pieces], refs[pieces:]
    half = chunks // 2
    router_ref, back_bias_ref, w_in, w_back, *refs = refs
    blocks, refs = refs[: pieces - 1], refs[pieces - 1 :]
    hidden_out, d_pre_out, d_results, d_rows_out, mixed_out, router_grad, back_bias_out = refs[:7]
    (
        ups_wide, marks, in_weight, back_weight, in_bias, results, d_rows, sems
    ) = refs[7:]
    piece = pl.program_id(0)

    def weight_copies_of(k):
        slot = k % 2
        if k == 0:
            sources = w_in.at[s_ref[5]], w_back.at[s_ref[5]]
        else:
            block = blocks[k - 1]
            sources = block.at[pl.ds(0, D)], block.at[pl.ds(D, hidden_width)]
        return [
            pltpu.make_async_copy(sources[0], in_weight.at[slot], sems.at[0, slot]),
            pltpu.make_async_copy(sources[1], back_weight.at[slot], sems.at[1, slot]),
        ]

    def start(k):
        for copy in weight_copies_of(k):
            copy.start()

    expert, first = s_ref[1], s_ref[2]
    rows = rows_in[...]
    label = lax.broadcasted_iota(jnp.int32, (1, EXPERTS), 1)
    mine = label == expert

    @pl.when(piece == 0)
    def _():
        start(0)
        for chunk in range(chunks):
            at = pl.multiple_of(jnp.bitwise_xor(s_ref[3], chunk) * CAP, 8)
            if chunk == half - 1:
                came = ups_in[-1][UPS:, :].astype(F32)
            else:
                came = ups_in[chunk if chunk < half else chunk - 1][0:UPS, :].astype(F32)
            ups_wide[pl.ds(at, CAP), :D] = came[:CAP]
            column = jnp.transpose(came[CAP:, :LANES])[:CAP, 0:1]
            ups_wide[pl.ds(at, CAP), D:] = jnp.broadcast_to(column, (CAP, LANES))
        lines = hidden_width // width
        for k in range(pieces):
            block = biases[k][...].astype(F32)
            bias_rows = block[0:lines]
            for e in range(1, block.shape[0] // lines):
                here = block[e * lines : (e + 1) * lines]
                bias_rows = jnp.where(s_ref[5] == e, here, bias_rows)
            for line in range(lines):
                in_bias[k : k + 1, line * width : (line + 1) * width] = bias_rows[line : line + 1]
        other = ups_wide[:, D : D + 1]
        logits = nt(rows, router_ref[...])
        others = label.astype(F32) == other
        own_logit = jnp.sum(jnp.where(mine, logits, 0.0), axis=1, keepdims=True)
        other_logit = jnp.sum(jnp.where(others, logits, 0.0), axis=1, keepdims=True)
        peak = jnp.maximum(own_logit, other_logit)
        own_exp, other_exp = jnp.exp(own_logit - peak), jnp.exp(other_logit - peak)
        gate = own_exp / (own_exp + other_exp)
        other_gate = other_exp / (own_exp + other_exp)
        lane = lax.broadcasted_iota(jnp.int32, (1, LANES), 1)
        marks[...] = jnp.where(lane == 0, gate, other_gate)
        d_results[...] = (gate * ups_wide[:, :D]).astype(BF16)
        results[...] = jnp.zeros_like(results)
        d_rows[...] = jnp.zeros_like(d_rows)

    for k in range(pieces):
        @pl.when(piece == k)
        def _():
            for copy in weight_copies_of(k):
                copy.wait()
            if k + 1 < pieces:
                start(k + 1)

    slot = lax.rem(piece, 2)
    in_now, back_now = in_weight[slot], back_weight[slot]
    pre_act = nn(rows, in_now) + in_bias[pl.ds(piece, 1), :]
    cdf = 0.5 * (1.0 + lax.erf(pre_act * (0.5**0.5)))
    hidden = (pre_act * cdf).astype(BF16)
    hidden_out[0] = hidden
    results[...] += nn(hidden, back_now)
    slope = cdf + pre_act * jnp.exp(-0.5 * pre_act * pre_act) * 0.3989422804014327
    d_pre = (slope * nt(d_results[...], back_now)).astype(BF16)
    d_pre_out[0] = d_pre
    d_rows[...] += nt(d_pre, in_now)

    @pl.when(piece == pieces - 1)
    def _():
        gate, other_gate = marks[:, 0:1], marks[:, 1:2]
        others = label.astype(F32) == ups_wide[:, D : D + 1]
        bias = jnp.where(first > 0, 1.0, 0.0) * back_bias_ref[...].astype(F32)
        pick = (lax.broadcasted_iota(jnp.int32, (EXPERTS, 1), 0) == expert).astype(F32)
        total = results[...] + jnp.sum(pick * bias, axis=0, keepdims=True)
        d_gate = jnp.sum(ups_wide[:, :D] * total, axis=1, keepdims=True)
        moved = gate * other_gate * d_gate
        d_logits = jnp.where(mine, moved, jnp.where(others, -moved, 0.0)).astype(BF16)
        router_grad[...] = tn(d_logits, rows)
        back_bias_out[...] = jnp.broadcast_to(
            jnp.sum(d_results[...].astype(F32), axis=0, keepdims=True), back_bias_out.shape
        )
        d_rows_out[...] = (d_rows[...] + nn(d_logits, router_ref[...])).astype(BF16)
        mixed_out[...] = (gate * total).astype(BF16)


def expert_grads_kernel(pieces, cuts, s_ref, rows_ref, d_ref, hiddens, d_pres, *refs):
    grads, sums = refs[:-1], refs[-1]
    hidden_width = hiddens.shape[2]
    sums[...] = jnp.zeros_like(sums)
    rows, d_results = rows_ref[...], d_ref[...]

    def step(index, carry):
        piece = jnp.int32(pieces[0])
        for k in range(1, len(pieces)):
            piece = jnp.where(index == k, pieces[k], piece)
        d_pre = d_pres[piece]
        in_grad = tn(rows, d_pre)
        back_grad = tn(hiddens[piece], d_results)
        bias_grad = jnp.sum(d_pre.astype(F32), axis=0, keepdims=True)
        sums[1:2, :] += jnp.sum(in_grad * in_grad)
        sums[2:3, :] += jnp.sum(bias_grad * bias_grad)
        sums[3:4, :] += jnp.sum(back_grad * back_grad)
        parts = (in_grad, jnp.broadcast_to(bias_grad, (16, hidden_width)), back_grad)
        for k in range(len(pieces)):
            @pl.when(index == k)
            def _():
                at = 0
                for part in parts:
                    done = 0
                    while done < part.shape[0]:
                        place, start = 0, at
                        while start >= cuts[place]:
                            start -= cuts[place]
                            place += 1
                        size = min(part.shape[0] - done, cuts[place] - start)
                        grads[k * len(cuts) + place][start : start + size, :] = part[
                            done : done + size
                        ].astype(BF16)
                        done += size
                        at += size

        return carry

    lax.fori_loop(0, len(pieces), step, 0)


def mixture_kernel(s_ref, middle_ref, part_ref, near_ref, out_ref):
    tokens = middle_ref.shape[0]
    total = part_ref[...].astype(F32) + near_ref[...].astype(F32)
    out_ref[0:tokens, :] = (total[0:tokens] + middle_ref[...].astype(F32)).astype(BF16)
    out_ref[tokens:, :] = total[tokens:].astype(BF16)


def output_kernel(images, groups, s_ref, middle_ref, part_ref, mask_ref, *refs):
    fars, (out_ref, sums, mask_pad) = refs[: groups // 2 - 1], refs[groups // 2 - 1 :]
    tokens = images * PAD
    for r in range(0, groups, 2):
        total = part_ref[r // 2 * tokens : (r // 2 + 1) * tokens, :].astype(F32)
        for far, ref in enumerate(fars, 1):
            at = ((r // 2) ^ far) * tokens
            total = total + ref[at : at + tokens, :].astype(F32)
        out_ref[r // 2 * tokens : (r // 2 + 1) * tokens, :] = total.astype(BF16)
        if r == 0:
            output = total
    mixture = output - middle_ref[...].astype(F32)
    valid = valid_column(images, key_masks(images, s_ref[0], mask_ref, mask_pad))
    lane = lax.broadcasted_iota(jnp.int32, sums.shape, 1)
    sums[...] = jnp.where(
        lane == 2, jnp.sum(mixture * mixture * valid),
        jnp.where(lane == 3, jnp.sum(output * output * valid), 0.0),
    )


def place_tokens_kernel(count, images, places, s_ref, *refs):
    out, wide = refs[-2:]
    for group, (index, place) in enumerate(places):
        for image in range(images):
            start = (place * images + image) * PAD
            rows = refs[index][start : start + PAD, :].astype(F32)[:SEQ]
            at = jnp.bitwise_xor(s_ref[0], group) * images + image
            for k in range(D // LANES):
                wide[k, pl.ds(at, SEQ, stride=count), :] = rows[:, k * LANES : (k + 1) * LANES]
    for k in range(D // LANES):
        out[:, k * LANES : (k + 1) * LANES] = wide[k]


def place_experts_kernel(counts, first_row, s_ref, *refs):
    ins, outs = refs[: sum(counts)], refs[-1 if first_row else -2 :]
    height = outs[0].shape[1]
    at = 0
    for step, count in enumerate(counts):
        parts, at = ins[at : at + count], at + count

        @pl.when(pl.program_id(0) == step)
        def _():
            row = 0
            for part in parts:
                begin, end = max(first_row, row), min(first_row + height, row + part.shape[0])
                if begin < end:
                    outs[0][0, begin - first_row : end - first_row, :] = part[
                        begin - row : end - row, :
                    ].astype(F32)
                row += part.shape[0]
            if not first_row:
                bias = parts[0][height : height + 16, :].astype(F32)[0:1, :]
                outs[1][...] = jnp.broadcast_to(bias, outs[1].shape)


def split_kernel(chunks, s_ref, part_ref, near_ref, far_ref, out_ref):
    total = part_ref[...].astype(F32) + near_ref[...].astype(F32) + far_ref[...].astype(F32)
    share = total.shape[0] // chunks
    for chunk in range(chunks):
        out_ref[chunk] = total[chunk * share : (chunk + 1) * share].astype(BF16)


def join_kernel(dims, s_ref, pieces_ref, *refs):
    chunks, groups, half, width, small = dims
    norm1, norm2, forward, expert, back_bias, near_bias, far_bias = refs[:7]
    message, lines = refs[7:]
    total = pieces_ref[0].astype(F32)
    for chunk in range(1, chunks):
        total += pieces_ref[chunk].astype(F32)
    share = total.shape[0]
    row = lax.broadcasted_iota(jnp.int32, (share, 1), 0) + s_ref[3] * share
    squares = total * total
    lines[...] = jnp.zeros_like(lines)
    at = 0
    for source, index in ((norm1, 0), (norm1, 1), (norm2, 0), (norm2, 1), (norm2, 2)):
        lines[at : at + D // LANES, :] = as_lines(source[index : index + 1, :])
        at += D // LANES
    for part in (0, 2):
        for group in range(groups):
            biases, chunk = (near_bias, group) if group < half else (far_bias, group - half)
            line = biases[0:1, (3 * chunk + part) * width : (3 * chunk + part) * width + LANES]
            lines[pl.ds(at + jnp.bitwise_xor(s_ref[0], group), 1), :] = line
        at += groups
    lane = lax.broadcasted_iota(jnp.int32, (1, LANES), 1)
    terms = [
        jnp.sum(forward[0:1, :]),
        jnp.sum(forward[1:2, :]),
        0.0,
        0.0,
        jnp.sum(norm1[2:3, :]),
        jnp.sum(forward[2:3, :]) * (1.0 / D),
        jnp.sum(jnp.where(row < 3 * D, squares, 0.0)),
        jnp.sum(jnp.where((row >= 3 * D) & (row < 4 * D), squares, 0.0)),
        expert[1:2, 0:1],
        expert[2:3, 0:1],
        expert[3:4, 0:1],
    ]
    scalars = jnp.zeros((1, LANES), F32)
    for index, term in enumerate(terms):
        scalars = jnp.where(lane == index, term, scalars)
    lines[at : at + 1, :] = scalars
    lines[small - 8 : small - 8 + D // LANES, :] = as_lines(back_bias[0:1, :])
    values = lines[...]
    high = values.astype(BF16)
    low = (values - high.astype(F32)).astype(BF16)
    for chunk in range(chunks):
        message[chunk, 0:share, :] = total.astype(BF16)
        message[chunk, share : share + small, :] = high
        message[chunk, share + small :, :] = low


def spread_kernel(dims, s_ref, messages, outputs, qkv_out, out_out, sums, total):
    chunks, groups, width, small = dims
    share = messages.shape[1] - 2 * small
    summed = jnp.zeros((small, LANES), F32)
    at = small - 8
    for chunk in range(chunks):
        total[chunk * share : (chunk + 1) * share, :] = messages[chunk, 0:share, :].astype(F32)
        lines = messages[chunk, share : share + small, :].astype(F32) + messages[
            chunk, share + small :, :
        ].astype(F32)
        summed += lines
        sums[at : at + D // LANES, :] = lines[small - 8 : small - 8 + D // LANES]
        at += D // LANES
    sums[0 : small - 8, :] = summed[0 : small - 8]
    scalars = 5 * D // LANES + 2 * groups
    sums[scalars : scalars + 1, :] += outputs[0:1, :]
    per = EXPERTS // groups * (D // LANES)
    sums[at : at + per, :] = total[4 * D : 4 * D + per, :]
    qkv_out[...] = total[0 : 3 * D, :]
    for block in range(D // width):
        out_out[:, block * width : (block + 1) * width] = total[
            3 * D + block * width : 3 * D + (block + 1) * width, :
        ]


def finish_kernel(dims, s_ref, mine_ref, came_ref, *refs):
    chunks, groups, half, small, shared = dims
    gain1, shift1, gain2, shift2, out_bias, bias_out, router_out, back_out, norms_out, rms_out = refs
    per = D // LANES
    top = small - 8
    summed = mine_ref[0:top, :] + came_ref[0:top, :]
    squares = []
    for index, out in enumerate((gain1, shift1, gain2, shift2, out_bias)):
        block = summed[index * per : (index + 1) * per]
        squares.append(jnp.sum(block * block))
        out[...] = as_rows(block)
    at = 5 * per
    biases = summed[at : at + 2 * groups]
    place = lax.broadcasted_iota(jnp.int32, (groups, 1), 0) == s_ref[0]
    for part in range(2):
        lines = biases[part * groups : (part + 1) * groups]
        bias_out[part : part + 1, :] = jnp.sum(
            jnp.where(place, lines, 0.0), axis=0, keepdims=True
        )
    scalars = summed[at + 2 * groups : at + 2 * groups + 1]
    lane = lax.broadcasted_iota(jnp.int32, (1, LANES), 1)

    def scalar(index):
        return jnp.sum(jnp.where(lane == index, scalars, 0.0))

    share = EXPERTS // groups
    size = chunks * per + share * per
    for group in range(groups):
        source = mine_ref if group < half else came_ref
        start = top + (group if group < half else group - half) * size
        owner = jnp.bitwise_xor(s_ref[0], group)
        lane_expert = owner if shared else 0
        for chunk in range(chunks):
            line = as_rows(source[start + chunk * per : start + (chunk + 1) * per, :])
            back_out[pl.ds(chunk * s_ref[4] + lane_expert, 1), :] = line
        start += chunks * per
        router_rows = as_rows(source[start : start + share * per, :])
        for g in range(groups):
            @pl.when(owner == g)
            def _():
                router_out[g * share : (g + 1) * share, :] = router_rows
    router, back_bias = router_out[...], back_out[...]
    ordered = [
        squares[0], squares[1], scalar(6), jnp.sum(biases * biases), scalar(7), squares[4],
        squares[2], squares[3], jnp.sum(router * router), scalar(8), scalar(9), scalar(10),
        jnp.sum(back_bias * back_bias),
    ]
    norms = jnp.zeros((1, LANES), F32)
    for index, value in enumerate(ordered):
        norms = jnp.where(lane == index, value, norms)
    norms_out[...] = jnp.sqrt(norms)[:, :13]
    rms_out[...] = jnp.sqrt(scalars / (scalar(5) * D))[:, :5]


def shards(
    inputs, valid_mask, expert_ids, slot_ids, norm1_gain, norm1_bias, w_qkv, b_qv, w_out, b_out,
    norm2_gain, norm2_bias, w_router, w_in, b_in, w_back, b_back, cotangent, dp_size, tensor_size,
):
    count = inputs.shape[0]
    groups = tensor_size
    images = count // groups
    local_width = w_qkv.shape[2]
    heads = local_width // HD
    width = -(-local_width // LANES) * LANES
    local_experts, _, hidden_width = w_in.shape
    shared = local_experts == groups == 4
    pieces = groups if shared else 1
    chunks = dp_size
    rows = chunks * CAP
    own_tokens = images * PAD
    half = groups // 2
    data_at = lax.axis_index("dp").astype(jnp.int32)
    head_at = lax.axis_index("tensor").astype(jnp.int32)
    lane_expert = head_at if shared else jnp.int32(0)
    expert_at = data_at * local_experts + lane_expert
    first = jnp.int32(1) if shared else (head_at == 0).astype(jnp.int32)
    scalars = jnp.stack(
        [head_at, expert_at, first, data_at, jnp.int32(local_experts), lane_expert]
    )
    x_lines = jnp.transpose(inputs, (1, 0, 2)).reshape(SEQ * count, D)
    cot_lines = jnp.transpose(cotangent, (1, 0, 2)).reshape(SEQ * count, D)
    ids = jnp.transpose(expert_ids, (0, 2, 1))
    slots = jnp.transpose(slot_ids, (0, 2, 1))
    norms = jnp.stack([norm1_gain, norm1_bias, norm2_gain, norm2_bias, b_out]).astype(F32)
    router = jnp.transpose(w_router)
    last = [None]

    def call(kernel, ins, outs, **options):
        at = scalars if last[0] is None else after(scalars, last[0])
        got = run(kernel, at, ins, outs, **options)
        last[0] = got[0]
        return got

    def over(axis, size, value, by, *others):
        return swap(after(value, *others) if others else value, axis, size, by)

    def core(value, *others):
        return over("tensor", groups, value, 1, *others)

    def gather(value):
        parts = [value] + [None] * (groups - 1)
        for r in range(2, groups, 2):
            parts[r] = over("tensor", groups, value, r)
        for r in range(1, groups, 2):
            parts[r] = core(parts[r - 1])
        return parts

    def exchange(value, *others):
        value = after(value, *others) if others else value
        return lax.all_to_all(value.reshape(chunks, CAP, -1), "dp", 0, 0).reshape(rows, -1)

    fill = width - local_width
    qkv = jnp.pad(jnp.transpose(w_qkv, (1, 0, 2)), [(0, 0), (0, 0), (0, fill)])
    qkv = qkv.reshape(3 * D, width)
    out_rows = jnp.pad(w_out, [(0, fill), (0, 0)])
    qv_bias = jnp.pad(b_qv, [(0, 0), (0, fill)])
    bias_at = 4 * D + 16
    bias_lines = -(-(local_experts * hidden_width // width) // 16) * 16
    pack = call(
        functools.partial(pack_kernel, width),
        [qkv, out_rows, qv_bias, b_in], [((bias_at + bias_lines, width), BF16)], mib=58,
    )[0]
    packs = [pack, core(pack)] + [None] * (groups - 2)
    for r in range(2, groups, 2):
        packs[r] = over("tensor", groups, pack, r)

    block = D + hidden_width
    tall = D // LANES, SEQ * count, LANES
    got = call(
        functools.partial(start_kernel, (count, images, chunks, shared)),
        [ids, slots, cot_lines] + ([w_in, w_back] if shared else []),
        [((own_tokens, D), BF16)] + [((UPS, D), BF16)] * (chunks // 2)
        + [((chunks // 2 * UPS, D), BF16)]
        + (
            [((block, D), BF16)] * (pieces - 1) if shared else []
        ),
        left=(3, 4), mib=58,
        scratch=[
            pltpu.VMEM(tall, F32), pltpu.VMEM((own_tokens, D), F32),
            pltpu.VMEM((rows, D), F32), pltpu.VMEM((rows, LANES), F32),
            pltpu.VMEM((LANES, LANES), F32), pltpu.VMEM((chunks * UPS, D), F32),
            pltpu.SemaphoreType.DMA((6,)),
        ],
    )
    cot_own, ups, up_far = got[0], got[1 : 1 + chunks // 2], got[1 + chunks // 2]
    up_far = over("dp", chunks, up_far, chunks // 2)
    if shared:
        weights = [got[-3], over("tensor", groups, got[-2], 2), got[-1]]
    else:
        weights = []
    for r in range(2, groups, 2):
        packs[r + 1] = core(packs[r], cot_own)

    mask_pad = pltpu.VMEM((8, WIDE), jnp.int32)
    x_own, normed1, normed2, middle, forward_sums, projected, attended = call(
        functools.partial(heads_kernel, count, images, heads, width, groups),
        [x_lines, norms, valid_mask, *packs],
        [((own_tokens, D), BF16)] * 4 + [((8, D), F32)]
        + [((own_tokens, groups * 3 * width), BF16), ((own_tokens, groups * width), BF16)],
        scratch=[pltpu.VMEM(tall, F32), pltpu.VMEM((own_tokens, D), F32), mask_pad], mib=MIB_HEADS,
        stream=True,
    )
    half_heads = {
        which: [
            pl.BlockSpec((own_tokens, half * size * width), lambda step, s, at=which: (0, at))
            for size in (3, 1)
        ]
        for which in (0, 1)
    }

    tokens = [normed2, core(normed2)] + [None] * (groups - 2)
    early = chunks // 2 - 1
    ups = list(ups)
    for r in range(1, early):
        ups[r] = over("dp", chunks, ups[r], r, normed2)
    for r in range(2, groups, 2):
        tokens[r] = over("tensor", groups, normed2, r)
    turn = [up_far, *ups[1:early]]
    if shared:
        turn.append(weights[1])
    for r in range(2, groups, 2):
        tokens[r + 1] = core(tokens[r], *turn)
    if shared:
        weights[2] = over("tensor", groups, weights[2], 3, tokens[2])
        weights[0] = core(weights[0], tokens[2])
    flat_pad = pltpu.VMEM((8, WIDE), jnp.int32)
    sent, *passed = call(
        functools.partial(dispatch_kernel, groups, images, chunks),
        [ids, slots, *tokens, up_far, ups[early]],
        [((rows, D), BF16)] + [((UPS, D), BF16)] * (early - 1) + [((2 * UPS, D), BF16)],
        scratch=[flat_pad],
    )
    dispatched = exchange(sent)
    passed = [over("dp", chunks, value, r) for r, value in enumerate(passed, 1)]
    ups = [*ups[:early], up_far, *passed]

    by_piece = pl.BlockSpec((1, rows, hidden_width), lambda step, s: (step, 0, 0))
    bias_spec = pl.BlockSpec((bias_lines, width), lambda step, s: (bias_at // bias_lines, 0))
    first_rows = pl.BlockSpec((UPS, D), lambda step, s: (0, 0))
    before = chunks
    hidden, d_pre, d_results, d_sent, mixed_sent, router_part, back_bias = call(
        functools.partial(expert_kernel, (chunks, pieces, hidden_width, width)),
        [dispatched, *ups, *packs[:pieces], router, b_back, w_in, w_back]
        + weights,
        [((pieces, rows, hidden_width), BF16)] * 2 + [((rows, D), BF16)] * 3
        + [((EXPERTS, D), F32), ((8, D), F32)],
        grid=(pieces,),
        in_specs={chunks // 2: first_rows, **{before + k: bias_spec for k in range(pieces)}},
        out_specs={0: by_piece, 1: by_piece},
        scratch=[
            pltpu.VMEM((rows, D + LANES), F32),
            pltpu.VMEM((rows, LANES), F32),
            pltpu.VMEM((2, D, hidden_width), BF16),
            pltpu.VMEM((2, hidden_width, D), BF16),
            pltpu.VMEM((8, hidden_width), F32),
            pltpu.VMEM((rows, D), F32),
            pltpu.VMEM((rows, D), F32),
            pltpu.SemaphoreType.DMA((2, 2)),
        ],
        left=range(before + pieces + 2, before + pieces + 4 + pieces), mib=61,
    )
    d_back = exchange(d_sent)
    tall_grad = D + 16 + hidden_width
    first_cut = -(-2 * tall_grad // 48) * 16
    plans = [((3,), (first_cut, tall_grad - first_cut)), ((2, 0, 1), (tall_grad,))]
    if not shared:
        plans = [((0,), (D + 16, hidden_width))]
    lane_counts = (D, D) if shared else (hidden_width, D)
    grads, expert_sums = {}, []
    for kept, cuts in plans:
        part = pl.BlockSpec(
            (1 if len(kept) == 1 else 3, rows, hidden_width),
            lambda step, s, at=kept[0] if len(kept) == 1 else 0: (at, 0, 0),
        )
        held = tuple(range(len(kept))) if len(kept) == 1 else kept
        *some, sums = call(
            functools.partial(expert_grads_kernel, held, cuts),
            [dispatched, d_results, hidden, d_pre],
            [((cut, wide), BF16) for cut, wide in zip(cuts, lane_counts)] * len(kept)
            + [((8, LANES), F32)],
            in_specs={2: part, 3: part}, mib=58,
        )
        for index, piece in enumerate(kept):
            grads[piece] = some[index * len(cuts) : (index + 1) * len(cuts)]
        expert_sums.append(sums)

    def combine(value):
        return call(
            functools.partial(combine_kernel, groups, images, chunks),
            [ids, slots, value],
            [((half * own_tokens, D), BF16)] * 2, scratch=[flat_pad],
        )

    def reduce_own(keep, send, size, *others):
        came = core(send)
        far = [None, None]
        for r in range(2, groups, 2):
            for part in range(2):
                start = r // 2 * size + part * (size // 2)
                span = slice(start, start + size // 2)
                out = (keep[span].astype(F32) + came[span].astype(F32)).astype(BF16)
                term = over("tensor", groups, out, r, *others)
                if far[part] is not None:
                    term = far[part].astype(F32) + term.astype(F32)
                far[part] = term
        return keep, came, far

    if shared:
        last_top = over("tensor", groups, grads[3][0], 2)
        d_back = after(d_back, last_top)
    d_keep, d_near, d_far = reduce_own(*combine(d_back), own_tokens)
    if shared:
        last_rest = over("tensor", groups, grads[3][1], 2, *d_far)
    mixed = exchange(mixed_sent, d_back)

    router_lines = EXPERTS // groups * (D // LANES)
    share = -(-(4 * D + router_lines) // (16 * chunks)) * 16

    def grads_out(parts):
        return [((8, parts * 3 * width), F32)] + [((chunks * share, width), BF16)] * parts

    first_half = pl.BlockSpec((own_tokens, D), lambda step, s: (0, 0))
    got = call(
        functools.partial(
            middle_pull_kernel, (images, heads, width, groups - half, half, groups)
        ),
        [cot_own, d_keep, d_near, *d_far, middle, norms, normed1, valid_mask, projected,
         attended, router_part, *packs[half:]],
        [((own_tokens, D), BF16), ((8, D), F32), ((own_tokens, D), BF16)]
        + grads_out(groups - half),
        scratch=[mask_pad], mib=MIB_PULL, in_specs={**dict(zip((9, 10), half_heads[1])), 1: first_half, 2: first_half},
    )
    d_low, norm2_sums, d_branch, far_bias = got[:4]
    far_grads = list(got[4:])

    def add_odd(grads):
        return (grads[0].astype(F32) + core(grads[1]).astype(F32)).astype(BF16)

    if shared:
        far_grads[1] = after(far_grads[1], last_rest)
    far = None
    for r in range(0, groups - half, 2):
        out = add_odd(far_grads[r : r + 2])
        d_low = after(d_low, out)
        term = over("tensor", groups, out, half + r)
        far = term if far is None else far.astype(F32) + term.astype(F32)
    got = call(
        functools.partial(input_pull_kernel, (images, heads, width, half, 0, groups)),
        [x_own, d_low, d_branch, norms, normed1, valid_mask, projected, attended,
         router_part, *packs[:half]],
        [((own_tokens, D), BF16), ((8, D), F32)] + grads_out(half),
        scratch=[mask_pad], mib=MIB_PULL, in_specs=dict(zip((6, 7), half_heads[0])),
    )
    d_own, norm1_sums, near_bias = got[:3]
    head_grads = list(got[3:])
    for r in range(2, half, 2):
        term = over("tensor", groups, add_odd(head_grads[r : r + 2]), r)
        far = far.astype(F32) + term.astype(F32)
    near = core(head_grads[1], far)
    split = call(
        functools.partial(split_kernel, chunks),
        [head_grads[0], near, far], [((chunks, share, width), BF16)],
    )[0]
    d_tokens = [d_own, core(d_own)] + [None] * (groups - 2)
    for r in range(2, groups, 2):
        d_tokens[r] = over("tensor", groups, d_own, r)
    pieces_in = lax.all_to_all(after(split, d_tokens[2]), "dp", 0, 0)
    mix_keep, mix_send = combine(mixed)
    mix_near = core(mix_send)

    def place_tokens(parts, places):
        placed = call(
            functools.partial(place_tokens_kernel, count, images, places),
            parts, [((SEQ * count, D), F32)],
            scratch=[pltpu.VMEM(tall, F32)],
        )[0]
        return jnp.transpose(placed.reshape(SEQ, count, D), (1, 0, 2))

    for r in range(2, groups, 2):
        d_tokens[r + 1] = core(d_tokens[r], split)

    def place_experts(came, pieces_here, first_row, shape, before=()):
        steps = len(pieces_here)

        def piece_at(step):
            place = jnp.int32(0)
            for index, piece in enumerate(pieces_here):
                place = jnp.where(step == index, piece, place)
            return place

        spec = pl.BlockSpec((1, *shape), lambda step, s: (jnp.bitwise_xor(s[0], piece_at(step)), 0, 0))
        lines = pl.BlockSpec((1, 8, hidden_width), lambda step, s: (step, 0, 0))
        parts = [a for piece in came for a in piece]
        bias = [] if first_row else [((steps, 8, hidden_width), F32)]
        return call(
            functools.partial(
                place_experts_kernel, tuple(len(piece) for piece in came), first_row
            ),
            [*parts, *before], [((local_experts, *shape), F32)] + bias,
            grid=(steps,), out_specs={0: spec, 1: lines}, left=range(len(parts), len(parts) + 1),
            aliases={len(parts): 0} if before else None,
        )

    mix = call(
        mixture_kernel, [middle, mix_keep, mix_near], [((half * own_tokens, D), BF16)]
    )[0]
    mix_far = [over("tensor", groups, mix, r) for r in range(2, groups, 2)]
    d_inputs = place_tokens(d_tokens, [(r, 0) for r in range(groups)])
    if shared:
        whole = (0, 1, 3), [grads[0], [core(grads[1][0])], [core(last_top), core(last_rest)]]
        g_w_in, lines_in = place_experts(whole[1], whole[0], 0, (D, hidden_width))
        (g_w_back,) = place_experts(whole[1], whole[0], D + 16, (hidden_width, D))
    small = -(-(5 * D // LANES + 2 * groups + 1) // 8) * 8 + 8
    small = -(-small // 16) * 16
    message = call(
        functools.partial(join_kernel, (chunks, groups, half, width, small)),
        [pieces_in, norm1_sums, norm2_sums, forward_sums, sum(expert_sums), back_bias, near_bias,
         far_bias],
        [((chunks, share + 2 * small, width), BF16)], scratch=[pltpu.VMEM((small, LANES), F32)],
        mib=58,
    )[0]
    messages = lax.all_to_all(message, "dp", 0, 0)
    output_own, output_sums = call(
        functools.partial(output_kernel, images, groups),
        [middle, mix, valid_mask, *mix_far],
        [((half * own_tokens, D), BF16), ((8, LANES), F32)], scratch=[mask_pad],
    )
    by = 1
    while by < chunks:
        output_sums = output_sums + over("dp", chunks, output_sums, by)
        by *= 2
    out_near = core(output_own)

    output = place_tokens([output_own, out_near], [(r % 2, r // 2) for r in range(groups)])
    top = small - 8
    qkv_sum, out_sum, sums = call(
        functools.partial(spread_kernel, (chunks, groups, width, small)),
        [messages, output_sums],
        [((3 * D, width), F32), ((width, D), F32),
         ((top + chunks * (D // LANES) + router_lines, LANES), F32)],
        scratch=[pltpu.VMEM((chunks * share, width), F32)],
    )
    by = 1
    while True:
        came = over("tensor", groups, sums, by)
        by *= 2
        if by == groups:
            break
        sums = jnp.concatenate([sums[:top] + came[:top], sums[top:], came[top:]], axis=0)

    if shared:
        last_piece = [[over("tensor", groups, grads[2][0], 2, mix_far[0])]]
        g_w_in, line_in = place_experts(last_piece, (2,), 0, (D, hidden_width), [g_w_in])
        (g_w_back,) = place_experts(last_piece, (2,), D + 16, (hidden_width, D), [g_w_back])
        by_piece = jnp.concatenate([lines_in[:2, 0], line_in[:, 0], lines_in[2:, 0]], axis=0)
        order = jnp.bitwise_xor(head_at, jnp.arange(groups, dtype=jnp.int32))
        g_b_in = jnp.take(by_piece, order, axis=0)
    else:
        g_w_in = grads[0][0][None, :D].astype(F32)
        g_w_back = grads[0][1][None].astype(F32)
        g_b_in = grads[0][0][D : D + 1].astype(F32)

    vector = [((1, D), F32)]
    (
        g_norm1_gain, g_norm1_bias, g_norm2_gain, g_norm2_bias, g_b_out, g_b_qv, router_grad,
        g_b_back, grad_norms, rms_values,
    ) = call(
        functools.partial(finish_kernel, (chunks, groups, half, small, shared)),
        [sums, came],
        vector * 5
        + [((2, LANES), F32), ((EXPERTS, D), F32), ((EXPERTS, D), F32)]
        + [((1, 13), F32), ((1, 5), F32)],
    )
    g_w_qkv = jnp.transpose(qkv_sum.reshape(3, D, width), (1, 0, 2))[:, :, :local_width]
    return (
        output, d_inputs, g_norm1_gain[0], g_norm1_bias[0], g_w_qkv, g_b_qv[:, :local_width],
        out_sum[:local_width], g_b_out[0], g_norm2_gain[0], g_norm2_bias[0],
        jnp.transpose(router_grad), g_w_in, g_b_in, g_w_back, g_b_back,
        grad_norms[0], rms_values[0],
    )


def solution(mesh):
    placed = (
        P("dp", None, None),
        P("dp", None),
        P("dp", None, None),
        P("dp", None, None),
        P(),
        P(),
        P(None, None, "tensor"),
        P(None, "tensor"),
        P("tensor", None),
        P(),
        P(),
        P(),
        P(),
        P("dp", None, "tensor"),
        P("dp", "tensor"),
        P("dp", "tensor", None),
        P(),
        P("dp", None, None),
    )
    return jax.shard_map(
        functools.partial(shards, dp_size=mesh.shape["dp"], tensor_size=mesh.shape["tensor"]),
        mesh=mesh,
        in_specs=placed,
        out_specs=(
            P("dp", None, None),
            P("dp", None, None),
            P(),
            P(),
            P(None, None, "tensor"),
            P(None, "tensor"),
            P("tensor", None),
            P(),
            P(),
            P(),
            P(),
            P("dp", None, "tensor"),
            P("dp", "tensor"),
            P("dp", "tensor", None),
            P(),
            P(),
            P(),
        ),
        check_vma=False,
    )
```

profile of v0, /device:TPU:0, one launch (start us, length us, event | category | flops | bytes accessed | tf_op | source)
XLA Modules:
  0.0 263.3 jit_solution(6584900075049163944)
XLA Ops:
  6.8 9.1 %shard_map.306 = (bf16[416,512]{1,0:T(8,128)(2,1)}, bf16[112,512]{1,0:T(8,128)(2,1)}, bf16[112,512]{1,0:T(8,128)(2,1)}, bf16[112,512]{1,0:T(8,128)(2,1)}, bf16[1...) custom-call(s32[6]{0:T(128)} %stack.34.s_ref, ...), custom_call_target="tpu_custom_call" | custom-call | tf_op jit(solution)/shard_map/pallas_call | solution.py:119
  16.1 3.6 %collective-permute-done.1.refs_5_.refs_9_.refs_0_ = bf16[2080,128]{1,0:T(8,128)(2,1)S(1)} collective-permute-done((bf16[2080,128]{1,0:T(8,128)(2,1)}, bf16[2080,128]{1,0:T(8,128)(2,1)S(1)}, u32[]{:S(2)}, u32[]{:S(2)}) %collective-permute-start.1) | collective-permute-done | bytes 532512 | tf_op jit(solution)/shard_map/ppermute | solution.py:40
  24.6 7.3 %shard_map.307 = (bf16[416,512]{1,0:T(8,128)(2,1)}, bf16[416,512]{1,0:T(8,128)(2,1)}, bf16[416,512]{1,0:T(8,128)(2,1)}, bf16[416,512]{1,0:T(8,128)(2,1)}, f32[8,...) custom-call(s32[6]{0:T(128)} %stack.34.s_ref, bf16[1576,512]{1,0:T(8,128)(2,1)} %bitcast.63, ...), custom_call_target="tpu_custom_call" | custom-call | tf_op jit(solution)/shard_map/pallas_call | solution.py:119
  36.9 7.3 %collective-permute-done.5.refs_4_.refs_3_ = bf16[448,512]{1,0:T(8,128)(2,1)S(1)} collective-permute-done((bf16[448,512]{1,0:T(8,128)(2,1)}, bf16[448,512]{1,0:T(8,128)(2,1)S(1)}, u32[]{:S(2)}, u32[]{:S(2)}) %collective-permute-start.5) | collective-permute-done | bytes 458784 | tf_op jit(solution)/shard_map/ppermute | solution.py:40
  46.5 4.2 %collective-permute-done.4.refs_2_ = bf16[416,512]{1,0:T(8,128)(2,1)S(1)} collective-permute-done((bf16[416,512]{1,0:T(8,128)(2,1)}, bf16[416,512]{1,0:T(8,128)(2,1)S(1)}, u32[]{:S(2)}, u32[]{:S(2)}) %collective-permute-start.4) | collective-permute-done | bytes 426016 | tf_op jit(solution)/shard_map/ppermute | solution.py:40
  56.9 6.1 %all-to-all-start = ((bf16[8,104,512]{2,1,0:T(8,128)(2,1)}), bf16[8,104,512]{2,1,0:T(8,128)(2,1)S(1)}, u32[]{:S(2)}, u32[]{:S(2)}) async-start(bf16[8,104,512]{2,1,0:T(8,128)(2,1)} %bitcast.11), calls=%async_computation | async-start | bytes 1703936 | tf_op jit(solution)/shard_map/all_to_all | solution.py:972
  68.1 7.5 %collective-permute-done.10.refs_4_ = bf16[112,512]{1,0:T(8,128)(2,1)S(1)} collective-permute-done((bf16[112,512]{1,0:T(8,128)(2,1)S(1)}, bf16[112,512]{1,0:T(8,128)(2,1)S(1)}, u32[]{:S(2)}, u32[]{:S(2)}) %collective-permute-start.10) | collective-permute-done | bytes 114720 | tf_op jit(solution)/shard_map/ppermute | solution.py:40
  75.6 11.2 %collective-permute-done.11.refs_5_ = bf16[112,512]{1,0:T(8,128)(2,1)S(1)} collective-permute-done((bf16[112,512]{1,0:T(8,128)(2,1)S(1)}, bf16[112,512]{1,0:T(8,128)(2,1)S(1)}, u32[]{:S(2)}, u32[]{:S(2)}) %collective-permute-start.11) | collective-permute-done | bytes 114720 | tf_op jit(solution)/shard_map/ppermute | solution.py:40
  89.2 17.0 %shard_map.309 = (bf16[4,832,512]{2,1,0:T(8,128)(2,1)}, bf16[4,832,512]{2,1,0:T(8,128)(2,1)}, bf16[832,512]{1,0:T(8,128)(2,1)}, bf16[832,512]{1,0:T(8,128)(2,1)}...) custom-call(s32[6]{0:T(128)} %stack.34.s_ref, bf16[832,512]{1,0:T(8,128)(2,1)} %bitcast.57, ...), custom_call_target="tpu_custom_call" | custom-call | tf_op jit(solution)/shard_map/pallas_call | solution.py:119
  106.2 5.9 %all-to-all-start.1 = ((bf16[8,104,512]{2,1,0:T(8,128)(2,1)}), bf16[8,104,512]{2,1,0:T(8,128)(2,1)S(1)}, u32[]{:S(2)}, u32[]{:S(2)}) async-start(bf16[8,104,512]{2,1,0:T(8,128)(2,1)} %bitcast.64), calls=%async_computation.1 | async-start | bytes 1703936 | tf_op jit(solution)/shard_map/all_to_all | solution.py:972
  112.1 4.9 %shard_map.310 = (bf16[704,512]{1,0:T(8,128)(2,1)}, bf16[336,512]{1,0:T(8,128)(2,1)}, f32[8,128]{1,0:T(8,128)}) custom-call(s32[6]{0:T(128)} %stack.34.s_ref, bf16[832,512]{1,0:T(8,128)(2,1)} %bitcast.58, bf16[832,512]{1,0:T(8,128)(2,1)} %get-tuple-element.149.d_ref, bf16[4,832,512]{2,1,0:T(8,128)(2,1)} %get-tuple-element.147.hiddens, ...), custom_call_target="tpu_custom_call" | custom-call | tf_op jit(solution)/shard_map/pallas_call | solution.py:119
  118.4 10.5 %shard_map.311 = (bf16[1040,512]{1,0:T(8,128)(2,1)}, bf16[1040,512]{1,0:T(8,128)(2,1)}, bf16[1040,512]{1,0:T(8,128)(2,1)}, f32[8,128]{1,0:T(8,128)}) custom-call(s32[6]{0:T(128)} %stack.34.s_ref, bf16[832,512]{1,0:T(8,128)(2,1)} %bitcast.59, bf16[832,512]{1,0:T(8,128)(2,1)} %get-tuple-element.149.d_ref, bf16[4,832,512]{2,1,0:T(8,128)(2,1)} %get-tuple-element.147.hiddens, ...), custom_call_target="tpu_custom_call" | custom-call | tf_op jit(solution)/shard_map/pallas_call | solution.py:119
  128.9 6.5 %collective-permute-done.15 = bf16[704,512]{1,0:T(8,128)(2,1)S(1)} collective-permute-done((bf16[704,512]{1,0:T(8,128)(2,1)}, bf16[704,512]{1,0:T(8,128)(2,1)S(1)}, u32[]{:S(2)}, u32[]{:S(2)}) %collective-permute-start.15) | collective-permute-done | bytes 720928 | tf_op jit(solution)/shard_map/ppermute | solution.py:40
  144.3 6.1 %collective-permute-done.17.top_ref = bf16[208,512]{1,0:T(8,128)(2,1)S(1)} collective-permute-done((bf16[208,512]{1,0:T(8,128)(2,1)S(1)}, bf16[208,512]{1,0:T(8,128)(2,1)S(1)}, u32[]{:S(2)}, u32[]{:S(2)}) %collective-permute-start.17) | collective-permute-done | bytes 213024 | tf_op jit(solution)/shard_map/ppermute | solution.py:40
  150.3 3.8 %collective-permute-done.18.rest_ref = bf16[208,512]{1,0:T(8,128)(2,1)S(1)} collective-permute-done((bf16[208,512]{1,0:T(8,128)(2,1)S(1)}, bf16[208,512]{1,0:T(8,128)(2,1)S(1)}, u32[]{:S(2)}, u32[]{:S(2)}) %collective-permute-start.18) | collective-permute-done | bytes 213024 | tf_op jit(solution)/shard_map/ppermute | solution.py:40
  155.6 8.5 %shard_map.313 = (bf16[416,512]{1,0:T(8,128)(2,1)}, f32[8,512]{1,0:T(8,128)}, bf16[416,512]{1,0:T(8,128)(2,1)}, f32[8,768]{1,0:T(8,128)}, bf16[2176,128]{1,0:T(8,128)(2,1)}, /*index=5*/bf16[2176,128]{1,0:T(8,128)(2,1)}) custom-call(s32[6]{0:T(128)} %stack.34.s_ref, bf16[416,512]{1,0:T(8,128)(2,1)} %get-tuple-element.123.cot_ref, bf16[832,512]{1,0:T(8,128)(2,1)} %copy-done.2, ...), custom_call_target="tpu_custom_call" | custom-call | tf_op jit(solution)/shard_map/pallas_call | solution.py:119
  165.0 5.7 %all-to-all-start.2 = ((bf16[8,104,512]{2,1,0:T(8,128)(2,1)}), bf16[8,104,512]{2,1,0:T(8,128)(2,1)S(1)}, u32[]{:S(2)}, u32[]{:S(2)}) async-start(bf16[8,104,512]{2,1,0:T(8,128)(2,1)} %bitcast.16), calls=%async_computation.2 | async-start | bytes 1703936 | tf_op jit(solution)/shard_map/all_to_all | solution.py:972
  171.6 8.4 %shard_map.314 = (bf16[416,512]{1,0:T(8,128)(2,1)}, f32[8,512]{1,0:T(8,128)}, f32[8,768]{1,0:T(8,128)}, bf16[2176,128]{1,0:T(8,128)(2,1)}, bf16[2176,128]{1,0:T(8,128)(2,1)}) custom-call(s32[6]{0:T(128)} %stack.34.s_ref, bf16[416,512]{1,0:T(8,128)(2,1)} %get-tuple-element.126.x_ref, bf16[416,512]{1,0:T(8,128)(2,1)} %get-tuple-element.172.d_normed_ref, ...), custom_call_target="tpu_custom_call" | custom-call | tf_op jit(solution)/shard_map/pallas_call | solution.py:119
  180.0 5.6 %collective-permute-done.21.far_ref = bf16[2176,128]{1,0:T(8,128)(2,1)S(1)} collective-permute-done((bf16[2176,128]{1,0:T(8,128)(2,1)S(1)}, bf16[2176,128]{1,0:T(8,128)(2,1)S(1)}, u32[]{:S(2)}, u32[]{:S(2)}) %collective-permute-start.21) | collective-permute-done | bytes 557088 | tf_op jit(solution)/shard_map/ppermute | solution.py:40
  192.9 4.3 %shard_map.316 = (bf16[832,512]{1,0:T(8,128)(2,1)S(1)}, bf16[832,512]{1,0:T(8,128)(2,1)}) custom-call(s32[6]{0:T(128)S(1)} %copy-done.11, s32[8,2,197]{2,1,0:T(2,128)S(1)} %bitcast.52, s32[8,2,197]{2,1,0:T(2,128)S(1)} %bitcast.56, bf16[832,512]{1,0:T(8,128)(2,1)S(1)} %bitcast.47), custom_call_target="tpu_custom_call" | custom-call | tf_op jit(solution)/shard_map/pallas_call | solution.py:119
  198.2 5.8 %all-to-all-start.3 = ((bf16[8,272,128]{2,1,0:T(8,128)(2,1)}), bf16[8,272,128]{2,1,0:T(8,128)(2,1)}, u32[]{:S(2)}, u32[]{:S(2)}) async-start(bf16[8,272,128]{2,1,0:T(8,128)(2,1)} %shard_map.315), calls=%async_computation.3 | async-start | bytes 1114112 | tf_op jit(solution)/shard_map/all_to_all | solution.py:1189
  209.0 4.6 %shard_map.318 = f32[1576,512]{1,0:T(8,128)} custom-call(s32[6]{0:T(128)S(1)} %copy-done.11, bf16[416,512]{1,0:T(8,128)(2,1)S(1)} %copy-done.7, bf16[416,512]{1,0:T(8,128)(2,1)S(1)} %collective-permute-done.24.refs_1_, bf16[416,512]{1,0:T(8,128)(2,1)} %collective-permute-done.25.refs_2_, bf16[416,512]{1,0:T(8,128)(2,1)S(1)} %collective-permute-done.26.refs_3_), custom_call_target="tpu_custom_call" | custom-call | tf_op jit(solution)/shard_map/pallas_call | solution.py:119
  222.2 6.0 %all-to-all-start.4 = ((bf16[8,368,128]{2,1,0:T(8,128)(2,1)}), bf16[8,368,128]{2,1,0:T(8,128)(2,1)S(1)}, u32[]{:S(2)}, u32[]{:S(2)}) async-start(bf16[8,368,128]{2,1,0:T(8,128)(2,1)} %shard_map.321), calls=%async_computation.4 | async-start | bytes 1507328 | tf_op jit(solution)/shard_map/all_to_all | solution.py:1244
  241.3 4.3 %collective-permute-start.34 = (f32[8,128]{1,0:T(8,128)S(1)}, f32[8,128]{1,0:T(8,128)S(1)}, u32[]{:S(2)}, u32[]{:S(2)}) collective-permute-start(f32[8,128]{1,0:T(8,128)S(1)} %add.48), channel_id=1, source_target_pairs={{0,16},{4,20},{8,24},{12,28},{16,0},{20,4},{24,8},{28,12},{1,17},{... | collective-permute-start | bytes 12296 | tf_op jit(solution)/shard_map/ppermute | solution.py:40
  (204 shorter events, 98.2 us)
Async XLA Ops:
  3.8 15.9 %collective-permute-start.1 = (bf16[2080,128]{1,0:T(8,128)(2,1)}, bf16[2080,128]{1,0:T(8,128)(2,1)S(1)}, u32[]{:S(2)}, u32[]{:S(2)}) collective-permute-start(bf16[2080,128]{1,0:T(8,128)(2,1)} %shard_map.305.refs_3_.refs_7_.refs_0_), channel_id=1, source_target_pairs={{0,2},{1,3},{2,0},{3,1},{4,6},{5,7},{6,4},{7,5},{8,10},{9,11},{10,... | collective-permute-start | bytes 1597448 | tf_op jit(solution)/shard_map/ppermute | solution.py:40
  15.9 28.2 %collective-permute-start.8 = (bf16[1024,512]{1,0:T(8,128)(2,1)}, bf16[1024,512]{1,0:T(8,128)(2,1)}, u32[]{:S(2)}, u32[]{:S(2)}) collective-permute-start(bf16[1024,512]{1,0:T(8,128)(2,1)} %get-tuple-element.134), channel_id=1, source_target_pairs={{0,2},{1,3},{2,0},{3,1},{4,6},{5,7},{6,4},{7,5},{8,10},{9,11},{10,... | collective-permute-start | bytes 3145736 | tf_op jit(solution)/shard_map/ppermute | solution.py:40
  19.7 24.4 %collective-permute-start.5 = (bf16[448,512]{1,0:T(8,128)(2,1)}, bf16[448,512]{1,0:T(8,128)(2,1)S(1)}, u32[]{:S(2)}, u32[]{:S(2)}) collective-permute-start(bf16[448,512]{1,0:T(8,128)(2,1)} %get-tuple-element.129), channel_id=1, source_target_pairs={{0,16},{4,20},{8,24},{12,28},{16,0},{20,4},{24,8},{28,12},{1,17},{... | collective-permute-start | bytes 1376264 | tf_op jit(solution)/shard_map/ppermute | solution.py:40
  32.0 18.7 %collective-permute-start.4 = (bf16[416,512]{1,0:T(8,128)(2,1)}, bf16[416,512]{1,0:T(8,128)(2,1)S(1)}, u32[]{:S(2)}, u32[]{:S(2)}) collective-permute-start(bf16[416,512]{1,0:T(8,128)(2,1)} %get-tuple-element.128.refs_0_), channel_id=1, source_target_pairs={{0,2},{1,3},{2,0},{3,1},{4,6},{5,7},{6,4},{7,5},{8,10},{9,11},{10,... | collective-permute-start | bytes 1277960 | tf_op jit(solution)/shard_map/ppermute | solution.py:40
  33.8 10.4 %collective-permute-start.6 = (bf16[112,512]{1,0:T(8,128)(2,1)S(1)}, bf16[112,512]{1,0:T(8,128)(2,1)S(1)}, u32[]{:S(2)}, u32[]{:S(2)}) collective-permute-start(bf16[112,512]{1,0:T(8,128)(2,1)S(1)} %copy-done.45), channel_id=1, source_target_pairs={{0,4},{4,0},{8,12},{12,8},{16,20},{20,16},{24,28},{28,24},{1,5},{5... | collective-permute-start | bytes 344072 | tf_op jit(solution)/shard_map/ppermute | solution.py:40
  35.3 11.2 %collective-permute-start.7 = (bf16[112,512]{1,0:T(8,128)(2,1)S(1)}, bf16[112,512]{1,0:T(8,128)(2,1)S(1)}, u32[]{:S(2)}, u32[]{:S(2)}) collective-permute-start(bf16[112,512]{1,0:T(8,128)(2,1)S(1)} %copy-done.44), channel_id=1, source_target_pairs={{0,8},{4,12},{8,0},{12,4},{16,24},{20,28},{24,16},{28,20},{1,9},{5... | collective-permute-start | bytes 344072 | tf_op jit(solution)/shard_map/ppermute | solution.py:40
  56.9 31.4 %all-to-all-start = ((bf16[8,104,512]{2,1,0:T(8,128)(2,1)}), bf16[8,104,512]{2,1,0:T(8,128)(2,1)S(1)}, u32[]{:S(2)}, u32[]{:S(2)}) async-start(bf16[8,104,512]{2,1,0:T(8,128)(2,1)} %bitcast.11), calls=%async_computation | async-start | bytes 1703936 | tf_op jit(solution)/shard_map/all_to_all | solution.py:972
  63.0 23.8 %collective-permute-start.13 = (bf16[1024,512]{1,0:T(8,128)(2,1)}, bf16[1024,512]{1,0:T(8,128)(2,1)S(1)}, u32[]{:S(2)}, u32[]{:S(2)}) collective-permute-start(bf16[1024,512]{1,0:T(8,128)(2,1)} %get-tuple-element.144), channel_id=1, source_target_pairs={{0,1},{1,0},{2,3},{3,2},{4,5},{5,4},{6,7},{7,6},{8,9},{9,8},{10,11... | collective-permute-start | bytes 3145736 | tf_op jit(solution)/shard_map/ppermute | solution.py:40
  63.0 25.3 %collective-permute-start.14 = (bf16[1024,512]{1,0:T(8,128)(2,1)}, bf16[1024,512]{1,0:T(8,128)(2,1)}, u32[]{:S(2)}, u32[]{:S(2)}) collective-permute-start(bf16[1024,512]{1,0:T(8,128)(2,1)} %get-tuple-element.146), channel_id=1, source_target_pairs={{0,3},{1,2},{2,1},{3,0},{4,7},{5,6},{6,5},{7,4},{8,11},{9,10},{10,... | collective-permute-start | bytes 3145736 | tf_op jit(solution)/shard_map/ppermute | solution.py:40
  64.6 22.2 %collective-permute-start.12 = (bf16[224,512]{1,0:T(8,128)(2,1)S(1)}, bf16[224,512]{1,0:T(8,128)(2,1)S(1)}, u32[]{:S(2)}, u32[]{:S(2)}) collective-permute-start(bf16[224,512]{1,0:T(8,128)(2,1)S(1)} %get-tuple-element.142), channel_id=1, source_target_pairs={{0,12},{4,8},{8,4},{12,0},{16,28},{20,24},{24,20},{28,16},{1,13},{... | collective-permute-start | bytes 688136 | tf_op jit(solution)/shard_map/ppermute | solution.py:40
  68.1 18.7 %collective-permute-start.11 = (bf16[112,512]{1,0:T(8,128)(2,1)S(1)}, bf16[112,512]{1,0:T(8,128)(2,1)S(1)}, u32[]{:S(2)}, u32[]{:S(2)}) collective-permute-start(bf16[112,512]{1,0:T(8,128)(2,1)S(1)} %get-tuple-element.141), channel_id=1, source_target_pairs={{0,8},{4,12},{8,0},{12,4},{16,24},{20,28},{24,16},{28,20},{1,9},{5... | collective-permute-start | bytes 344072 | tf_op jit(solution)/shard_map/ppermute | solution.py:40
  106.2 29.2 %all-to-all-start.1 = ((bf16[8,104,512]{2,1,0:T(8,128)(2,1)}), bf16[8,104,512]{2,1,0:T(8,128)(2,1)S(1)}, u32[]{:S(2)}, u32[]{:S(2)}) async-start(bf16[8,104,512]{2,1,0:T(8,128)(2,1)} %bitcast.64), calls=%async_computation.1 | async-start | bytes 1703936 | tf_op jit(solution)/shard_map/all_to_all | solution.py:972
  116.9 18.4 %collective-permute-start.15 = (bf16[704,512]{1,0:T(8,128)(2,1)}, bf16[704,512]{1,0:T(8,128)(2,1)S(1)}, u32[]{:S(2)}, u32[]{:S(2)}) collective-permute-start(bf16[704,512]{1,0:T(8,128)(2,1)} %get-tuple-element.151), channel_id=1, source_target_pairs={{0,2},{1,3},{2,0},{3,1},{4,6},{5,7},{6,4},{7,5},{8,10},{9,11},{10,... | collective-permute-start | bytes 2162696 | tf_op jit(solution)/shard_map/ppermute | solution.py:40
  143.8 10.3 %collective-permute-start.18 = (bf16[208,512]{1,0:T(8,128)(2,1)S(1)}, bf16[208,512]{1,0:T(8,128)(2,1)S(1)}, u32[]{:S(2)}, u32[]{:S(2)}) collective-permute-start(bf16[208,512]{1,0:T(8,128)(2,1)S(1)} %get-tuple-element.227), channel_id=1, source_target_pairs={{0,2},{1,3},{2,0},{3,1},{4,6},{5,7},{6,4},{7,5},{8,10},{9,11},{10,... | collective-permute-start | bytes 638984 | tf_op jit(solution)/shard_map/ppermute | solution.py:40
  154.1 10.1 %collective-permute-start.19 = (bf16[336,512]{1,0:T(8,128)(2,1)S(1)}, bf16[336,512]{1,0:T(8,128)(2,1)S(1)}, u32[]{:S(2)}, u32[]{:S(2)}) collective-permute-start(bf16[336,512]{1,0:T(8,128)(2,1)S(1)} %copy-done.43), channel_id=1, source_target_pairs={{0,2},{1,3},{2,0},{3,1},{4,6},{5,7},{6,4},{7,5},{8,10},{9,11},{10,... | collective-permute-start | bytes 1032200 | tf_op jit(solution)/shard_map/ppermute | solution.py:40
  165.0 27.9 %all-to-all-start.2 = ((bf16[8,104,512]{2,1,0:T(8,128)(2,1)}), bf16[8,104,512]{2,1,0:T(8,128)(2,1)S(1)}, u32[]{:S(2)}, u32[]{:S(2)}) async-start(bf16[8,104,512]{2,1,0:T(8,128)(2,1)} %bitcast.16), calls=%async_computation.2 | async-start | bytes 1703936 | tf_op jit(solution)/shard_map/all_to_all | solution.py:972
  170.8 14.8 %collective-permute-start.21 = (bf16[2176,128]{1,0:T(8,128)(2,1)S(1)}, bf16[2176,128]{1,0:T(8,128)(2,1)S(1)}, u32[]{:S(2)}, u32[]{:S(2)}) collective-permute-start(bf16[2176,128]{1,0:T(8,128)(2,1)S(1)} %add_convert_fusion), channel_id=1, source_target_pairs={{0,2},{1,3},{2,0},{3,1},{4,6},{5,7},{6,4},{7,5},{8,10},{9,11},{10,... | collective-permute-start | bytes 1671176 | tf_op jit(solution)/shard_map/ppermute | solution.py:40
  185.7 12.5 %collective-permute-start.25 = (bf16[416,512]{1,0:T(8,128)(2,1)}, bf16[416,512]{1,0:T(8,128)(2,1)}, u32[]{:S(2)}, u32[]{:S(2)}) collective-permute-start(bf16[416,512]{1,0:T(8,128)(2,1)} %get-tuple-element.174.refs_0_), channel_id=1, source_target_pairs={{0,2},{1,3},{2,0},{3,1},{4,6},{5,7},{6,4},{7,5},{8,10},{9,11},{10,... | collective-permute-start | bytes 1277960 | tf_op jit(solution)/shard_map/ppermute | solution.py:40
  197.1 16.5 %collective-permute-start.27 = (bf16[1040,512]{1,0:T(8,128)(2,1)}, bf16[1040,512]{1,0:T(8,128)(2,1)S(1)}, u32[]{:S(2)}, u32[]{:S(2)}) collective-permute-start(bf16[1040,512]{1,0:T(8,128)(2,1)} %get-tuple-element.189), channel_id=1, source_target_pairs={{0,1},{1,0},{2,3},{3,2},{4,5},{5,4},{6,7},{7,6},{8,9},{9,8},{10,11... | collective-permute-start | bytes 3194888 | tf_op jit(solution)/shard_map/ppermute | solution.py:40
  198.2 21.0 %all-to-all-start.3 = ((bf16[8,272,128]{2,1,0:T(8,128)(2,1)}), bf16[8,272,128]{2,1,0:T(8,128)(2,1)}, u32[]{:S(2)}, u32[]{:S(2)}) async-start(bf16[8,272,128]{2,1,0:T(8,128)(2,1)} %shard_map.315), calls=%async_computation.3 | async-start | bytes 1114112 | tf_op jit(solution)/shard_map/all_to_all | solution.py:1189
  207.5 21.5 %collective-permute-start.30 = (bf16[832,512]{1,0:T(8,128)(2,1)S(1)}, bf16[832,512]{1,0:T(8,128)(2,1)}, u32[]{:S(2)}, u32[]{:S(2)}) collective-permute-start(bf16[832,512]{1,0:T(8,128)(2,1)S(1)} %shard_map.317.part_ref), channel_id=1, source_target_pairs={{0,2},{1,3},{2,0},{3,1},{4,6},{5,7},{6,4},{7,5},{8,10},{9,11},{10,... | collective-permute-start | bytes 2555912 | tf_op jit(solution)/shard_map/ppermute | solution.py:40
  222.2 29.6 %all-to-all-start.4 = ((bf16[8,368,128]{2,1,0:T(8,128)(2,1)}), bf16[8,368,128]{2,1,0:T(8,128)(2,1)S(1)}, u32[]{:S(2)}, u32[]{:S(2)}) async-start(bf16[8,368,128]{2,1,0:T(8,128)(2,1)} %shard_map.321), calls=%async_computation.4 | async-start | bytes 1507328 | tf_op jit(solution)/shard_map/all_to_all | solution.py:1244
  231.4 16.8 %collective-permute-start.31 = (bf16[832,512]{1,0:T(8,128)(2,1)S(1)}, bf16[832,512]{1,0:T(8,128)(2,1)S(1)}, u32[]{:S(2)}, u32[]{:S(2)}) collective-permute-start(bf16[832,512]{1,0:T(8,128)(2,1)S(1)} %get-tuple-element.203.refs_0_), channel_id=1, source_target_pairs={{0,1},{1,0},{2,3},{3,2},{4,5},{5,4},{6,7},{7,6},{8,9},{9,8},{10,11... | collective-permute-start | bytes 2555912 | tf_op jit(solution)/shard_map/ppermute | solution.py:40
  231.5 25.9 %collective-permute-start.35 = (bf16[1040,512]{1,0:T(8,128)(2,1)S(1)}, bf16[1040,512]{1,0:T(8,128)(2,1)S(1)}, u32[]{:S(2)}, u32[]{:S(2)}) collective-permute-start(bf16[1040,512]{1,0:T(8,128)(2,1)S(1)} %copy-done.39), channel_id=1, source_target_pairs={{0,2},{1,3},{2,0},{3,1},{4,6},{5,7},{6,4},{7,5},{8,10},{9,11},{10,... | collective-permute-start | bytes 3194888 | tf_op jit(solution)/shard_map/ppermute | solution.py:40
  (65 other events, 574.6 us)
where the time goes:
time: 264 us; the launch traced here: 263 us
  Pallas kernels  107 us (41%)
  waiting for transfers between devices  78.5 us (30%)
  starting transfers between devices  64.7 us (25%)
  local copies, waits for them, and re-layouts  10.1 us (4%)
    pallas_call x23, Pallas kernels, run(): pl.pallas_call(kernel, grid_spec=pltpu.PrefetchScalarGridSpec(num_scalar_...  107 us
    ppermute x38, waiting for transfers between devices, swap(): return lax.ppermute(value, axis, [(at, at ^ by) for at in range(size)])  75.8 us
    ppermute x38, starting transfers between devices, swap(): return lax.ppermute(value, axis, [(at, at ^ by) for at in range(size)])  35.2 us
    all_to_all x3, starting transfers between devices, exchange(): lax.all_to_all(value.reshape(chunks, CAP, -1), 'dp', 0, 0).reshape(rows, -1)  17.7 us
    unnamed x93, local copies, waits for them, and re-layouts  8.82 us
    all_to_all x1, starting transfers between devices, shards(): messages = lax.all_to_all(message, 'dp', 0, 0)  5.98 us
    all_to_all x1, starting transfers between devices, shards(): pieces_in = lax.all_to_all(after(split, d_tokens[2]), 'dp', 0, 0)  5.84 us
  transfers between devices with their start and end apart: 43, of which 23 were waited for; matrix products, arithmetic and copies ran while one was open for 1% of the time, Pallas kernels for 30%

commit v1 on v0

--- a/solution.py
+++ b/solution.py
@@ -15,7 +15,7 @@
 PAD = 208
 UPS = CAP + 8
 WIDE = 256
-MIB_HEADS = 58
+MIB_HEADS = 52
 MIB_EXPERT = 58
 MIB_GRADS = 58
 MIB_PULL = 58
@@ -103,9 +103,11 @@
 
 def run(
     kernel, scalars, ins, outs, scratch=(), grid=(1,), in_specs=None, out_specs=None, mib=28, left=(),
-    stream=False, aliases=None,
+    stream=False, aliases=None, near=(),
 ):
     in_specs, out_specs = in_specs or {}, out_specs or {}
+    if len(near) == len(outs):
+        ins = [pltpu.with_memory_space_constraint(a, pltpu.HBM) for a in ins]
     if stream:
         kernel, scratch = streamed(kernel, ins, outs, scratch)
         left = range(len(ins))
@@ -128,7 +130,10 @@
             out_specs=[out_specs[i] if i in out_specs else whole(o[0]) for i, o in enumerate(outs)],
             scratch_shapes=list(scratch),
         ),
-        out_shape=[jax.ShapeDtypeStruct(shape, dtype) for shape, dtype in outs],
+        out_shape=[
+            (pltpu.VMEM if i in near else pltpu.HBM if near else jax.ShapeDtypeStruct)(*out)
+            for i, out in enumerate(outs)
+        ],
         input_output_aliases={i + 1: o for i, o in (aliases or {}).items()},
         compiler_params=pltpu.CompilerParams(vmem_limit_bytes=mib * 2**20),
         cost_estimate=pl.CostEstimate(flops=0, bytes_accessed=0, transcendentals=0),
@@ -694,7 +699,10 @@
         sums[2:3, :] += jnp.sum(bias_grad * bias_grad)
         sums[3:4, :] += jnp.sum(back_grad * back_grad)
         parts = (in_grad, jnp.broadcast_to(bias_grad, (16, hidden_width)), back_grad)
-        for k in range(len(pieces)):
+        first = 0
+        for k, heights in enumerate(cuts):
+            arrays, first = grads[first : first + len(heights)], first + len(heights)
+
             @pl.when(index == k)
             def _():
                 at = 0
@@ -702,13 +710,11 @@
                     done = 0
                     while done < part.shape[0]:
                         place, start = 0, at
-                        while start >= cuts[place]:
-                            start -= cuts[place]
+                        while start >= heights[place]:
+                            start -= heights[place]
                             place += 1
-                        size = min(part.shape[0] - done, cuts[place] - start)
-                        grads[k * len(cuts) + place][start : start + size, :] = part[
-                            done : done + size
-                        ].astype(BF16)
+                        size = min(part.shape[0] - done, heights[place] - start)
+                        arrays[place][start : start + size, :] = part[done : done + size].astype(BF16)
                         done += size
                         at += size
 
@@ -759,6 +765,7 @@
 
 def place_experts_kernel(counts, first_row, s_ref, *refs):
     ins, outs = refs[: sum(counts)], refs[-1 if first_row else -2 :]
+    lines = None if first_row or len(counts) > 1 else refs[sum(counts)]
     height = outs[0].shape[1]
     at = 0
     for step, count in enumerate(counts):
@@ -776,7 +783,13 @@
                 row += part.shape[0]
             if not first_row:
                 bias = parts[0][height : height + 16, :].astype(F32)[0:1, :]
-                outs[1][...] = jnp.broadcast_to(bias, outs[1].shape)
+                if lines is None:
+                    outs[1][...] = jnp.broadcast_to(bias, outs[1].shape)
+                else:
+                    for index, piece in enumerate((0, 1, 3)):
+                        owner = jnp.bitwise_xor(s_ref[0], piece)
+                        outs[1][pl.ds(owner, 1), :] = lines[index, 0:1, :]
+                    outs[1][pl.ds(jnp.bitwise_xor(s_ref[0], 2), 1), :] = bias
 
 
 def split_kernel(chunks, s_ref, part_ref, near_ref, far_ref, out_ref):
@@ -980,7 +993,7 @@
     bias_lines = -(-(local_experts * hidden_width // width) // 16) * 16
     pack = call(
         functools.partial(pack_kernel, width),
-        [qkv, out_rows, qv_bias, b_in], [((bias_at + bias_lines, width), BF16)], mib=58,
+        [qkv, out_rows, qv_bias, b_in], [((bias_at + bias_lines, width), BF16)], mib=48, near=(0,),
     )[0]
     packs = [pack, core(pack)] + [None] * (groups - 2)
     for r in range(2, groups, 2):
@@ -1020,7 +1033,7 @@
         [((own_tokens, D), BF16)] * 4 + [((8, D), F32)]
         + [((own_tokens, groups * 3 * width), BF16), ((own_tokens, groups * width), BF16)],
         scratch=[pltpu.VMEM(tall, F32), pltpu.VMEM((own_tokens, D), F32), mask_pad], mib=MIB_HEADS,
-        stream=True,
+        stream=True, near=(2,),
     )
     half_heads = {
         which: [
@@ -1084,9 +1097,11 @@
     d_back = exchange(d_sent)
     tall_grad = D + 16 + hidden_width
     first_cut = -(-2 * tall_grad // 48) * 16
-    plans = [((3,), (first_cut, tall_grad - first_cut)), ((2, 0, 1), (tall_grad,))]
+    two = first_cut, tall_grad - first_cut
+    most = tall_grad - 160, 160
+    plans = [((3,), (two,)), ((2, 0, 1), (most, (tall_grad,), (tall_grad,)))]
     if not shared:
-        plans = [((0,), (D + 16, hidden_width))]
+        plans = [((0,), ((D + 16, hidden_width),))]
     lane_counts = (D, D) if shared else (hidden_width, D)
     grads, expert_sums = {}, []
     for kept, cuts in plans:
@@ -1098,12 +1113,12 @@
         *some, sums = call(
             functools.partial(expert_grads_kernel, held, cuts),
             [dispatched, d_results, hidden, d_pre],
-            [((cut, wide), BF16) for cut, wide in zip(cuts, lane_counts)] * len(kept)
+            [((cut, wide), BF16) for heights in cuts for cut, wide in zip(heights, lane_counts)]
             + [((8, LANES), F32)],
             in_specs={2: part, 3: part}, mib=58,
         )
-        for index, piece in enumerate(kept):
-            grads[piece] = some[index * len(cuts) : (index + 1) * len(cuts)]
+        for piece, heights in zip(kept, cuts):
+            grads[piece], some = some[: len(heights)], some[len(heights) :]
         expert_sums.append(sums)
 
     def combine(value):
@@ -1181,7 +1196,7 @@
     near = core(head_grads[1], far)
     split = call(
         functools.partial(split_kernel, chunks),
-        [head_grads[0], near, far], [((chunks, share, width), BF16)],
+        [head_grads[0], near, far], [((chunks, share, width), BF16)], mib=58,
     )[0]
     d_tokens = [d_own, core(d_own)] + [None] * (groups - 2)
     for r in range(2, groups, 2):
@@ -1201,7 +1216,7 @@
     for r in range(2, groups, 2):
         d_tokens[r + 1] = core(d_tokens[r], split)
 
-    def place_experts(came, pieces_here, first_row, shape, before=()):
+    def place_experts(came, pieces_here, first_row, shape, before=[]):
         steps = len(pieces_here)
 
         def piece_at(step):
@@ -1214,18 +1229,24 @@
         lines = pl.BlockSpec((1, 8, hidden_width), lambda step, s: (step, 0, 0))
         parts = [a for piece in came for a in piece]
         bias = [] if first_row else [((steps, 8, hidden_width), F32)]
+        out_specs = {0: spec, 1: lines}
+        if not first_row and steps == 1:
+            bias, out_specs = [((local_experts, hidden_width), F32)], {0: spec}
         return call(
             functools.partial(
                 place_experts_kernel, tuple(len(piece) for piece in came), first_row
             ),
             [*parts, *before], [((local_experts, *shape), F32)] + bias,
-            grid=(steps,), out_specs={0: spec, 1: lines}, left=range(len(parts), len(parts) + 1),
-            aliases={len(parts): 0} if before else None,
+            grid=(steps,), out_specs=out_specs, left=[len(parts + before) - 1] if before else (),
+            aliases={len(parts + before) - 1: 0} if before else None,
         )
 
     mix = call(
-        mixture_kernel, [middle, mix_keep, mix_near], [((half * own_tokens, D), BF16)]
+        mixture_kernel, [middle, mix_keep, mix_near], [((half * own_tokens, D), BF16)], mib=58,
     )[0]
+    if shared:
+        piece_rest = over("tensor", groups, grads[2][1], 2, d_tokens[2])
+        mix = after(mix, piece_rest)
     mix_far = [over("tensor", groups, mix, r) for r in range(2, groups, 2)]
     d_inputs = place_tokens(d_tokens, [(r, 0) for r in range(groups)])
     if shared:
@@ -1247,13 +1268,14 @@
         [middle, mix, valid_mask, *mix_far],
         [((half * own_tokens, D), BF16), ((8, LANES), F32)], scratch=[mask_pad],
     )
-    by = 1
+    out_near = core(output_own)
+    output_sums = output_sums + over("dp", chunks, output_sums, 1)
+    output = place_tokens([output_own, out_near], [(r % 2, r // 2) for r in range(groups)])
+    output_sums = after(output_sums, output)
+    by = 2
     while by < chunks:
         output_sums = output_sums + over("dp", chunks, output_sums, by)
         by *= 2
-    out_near = core(output_own)
-
-    output = place_tokens([output_own, out_near], [(r % 2, r // 2) for r in range(groups)])
     top = small - 8
     qkv_sum, out_sum, sums = call(
         functools.partial(spread_kernel, (chunks, groups, width, small)),
@@ -1271,12 +1293,11 @@
         sums = jnp.concatenate([sums[:top] + came[:top], sums[top:], came[top:]], axis=0)
 
     if shared:
-        last_piece = [[over("tensor", groups, grads[2][0], 2, mix_far[0])]]
-        g_w_in, line_in = place_experts(last_piece, (2,), 0, (D, hidden_width), [g_w_in])
+        last_piece = [[over("tensor", groups, grads[2][0], 2, mix_far[0]), piece_rest]]
+        g_w_in, g_b_in = place_experts(
+            last_piece, (2,), 0, (D, hidden_width), [lines_in, g_w_in]
+        )
         (g_w_back,) = place_experts(last_piece, (2,), D + 16, (hidden_width, D), [g_w_back])
-        by_piece = jnp.concatenate([lines_in[:2, 0], line_in[:, 0], lines_in[2:, 0]], axis=0)
-        order = jnp.bitwise_xor(head_at, jnp.arange(groups, dtype=jnp.int32))
-        g_b_in = jnp.take(by_piece, order, axis=0)
     else:
         g_w_in = grads[0][0][None, :D].astype(F32)
         g_w_back = grads[0][1][None].astype(F32)

time: 264 us -> 257 us (0.973)
  local copies, waits for them, and re-layouts: 10.1 us -> 5.12 us
    unnamed x93 -> x92, local copies, waits for them, and re-layouts: 8.82 us -> 4.98 us
    ppermute x38 -> x39, waiting for transfers between devices: 75.8 us -> 75.9 us  [swap(): return lax.ppermute(value, axis, [(at, at ^ by) for at in range(size)])]
    ppermute x38 -> x39, starting transfers between devices: 35.2 us -> 35.1 us  [swap(): return lax.ppermute(value, axis, [(at, at ^ by) for at in range(size)])]
  transfers between devices with their start and end apart: 43 -> 44, of which waited for: 23 -> 22; matrix products, arithmetic and copies ran while one was open for 1% -> 1% of each run, Pallas kernels for 30% -> 32%
where the time goes in v1:
time: 257 us
  Pallas kernels  108 us (42%)
  waiting for transfers between devices  75.9 us (30%)
  starting transfers between devices  64.4 us (25%)
  local copies, waits for them, and re-layouts  5.12 us (2%)
    pallas_call x23, Pallas kernels, run(): pl.pallas_call(kernel, grid_spec=pltpu.PrefetchScalarGridSpec(num_scalar_...  108 us
    ppermute x39, waiting for transfers between devices, swap(): return lax.ppermute(value, axis, [(at, at ^ by) for at in range(size)])  75.9 us
    ppermute x39, starting transfers between devices, swap(): return lax.ppermute(value, axis, [(at, at ^ by) for at in range(size)])  35.1 us
    all_to_all x3, starting transfers between devices, exchange(): lax.all_to_all(value.reshape(chunks, CAP, -1), 'dp', 0, 0).reshape(rows, -1)  17.7 us
    all_to_all x1, starting transfers between devices, shards(): messages = lax.all_to_all(message, 'dp', 0, 0)  5.92 us
    all_to_all x1, starting transfers between devices, shards(): pieces_in = lax.all_to_all(after(split, d_tokens[2]), 'dp', 0, 0)  5.71 us
  transfers between devices with their start and end apart: 44, of which 22 were waited for; matrix products, arithmetic and copies ran while one was open for 1% of the time, Pallas kernels for 32%

profile of v1, /device:TPU:0, one launch (start us, length us, event | category | flops | bytes accessed | tf_op | source)
XLA Modules:
  0.0 256.6 jit_solution(4560649674472434673)
XLA Ops:
  5.5 9.1 %shard_map.306 = (bf16[416,512]{1,0:T(8,128)(2,1)}, bf16[112,512]{1,0:T(8,128)(2,1)}, bf16[112,512]{1,0:T(8,128)(2,1)}, bf16[112,512]{1,0:T(8,128)(2,1)}, bf16[1...) custom-call(s32[6]{0:T(128)} %copy-done.9, ...), custom_call_target="tpu_custom_call" | custom-call | tf_op jit(solution)/shard_map/pallas_call | solution.py:121
  21.9 7.5 %shard_map.307 = (bf16[416,512]{1,0:T(8,128)(2,1)}, bf16[416,512]{1,0:T(8,128)(2,1)}, bf16[416,512]{1,0:T(8,128)(2,1)S(1)}, bf16[416,512]{1,0:T(8,128)(2,1)}, f3...) custom-call(s32[6]{0:T(128)S(1)} %copy-done.10, bf16[1576,512]{1,0:T(8,128)(2,1)} %bitcast.54, ...), custom_call_target="tpu_custom_call" | custom-call | tf_op jit(solution)/shard_map/pallas_call | solution.py:121
  34.6 7.8 %collective-permute-done.5.refs_4_.refs_3_ = bf16[448,512]{1,0:T(8,128)(2,1)S(1)} collective-permute-done((bf16[448,512]{1,0:T(8,128)(2,1)}, bf16[448,512]{1,0:T(8,128)(2,1)S(1)}, u32[]{:S(2)}, u32[]{:S(2)}) %collective-permute-start.5) | collective-permute-done | bytes 458784 | tf_op jit(solution)/shard_map/ppermute | solution.py:40
  44.7 4.4 %collective-permute-done.4.refs_2_ = bf16[416,512]{1,0:T(8,128)(2,1)S(1)} collective-permute-done((bf16[416,512]{1,0:T(8,128)(2,1)S(1)}, bf16[416,512]{1,0:T(8,128)(2,1)S(1)}, u32[]{:S(2)}, u32[]{:S(2)}) %collective-permute-start.4) | collective-permute-done | bytes 426016 | tf_op jit(solution)/shard_map/ppermute | solution.py:40
  54.4 6.1 %all-to-all-start = ((bf16[8,104,512]{2,1,0:T(8,128)(2,1)}), bf16[8,104,512]{2,1,0:T(8,128)(2,1)S(1)}, u32[]{:S(2)}, u32[]{:S(2)}) async-start(bf16[8,104,512]{2,1,0:T(8,128)(2,1)} %bitcast.11), calls=%async_computation | async-start | bytes 1703936 | tf_op jit(solution)/shard_map/all_to_all | solution.py:985
  65.6 7.5 %collective-permute-done.10.refs_4_ = bf16[112,512]{1,0:T(8,128)(2,1)S(1)} collective-permute-done((bf16[112,512]{1,0:T(8,128)(2,1)S(1)}, bf16[112,512]{1,0:T(8,128)(2,1)S(1)}, u32[]{:S(2)}, u32[]{:S(2)}) %collective-permute-start.10) | collective-permute-done | bytes 114720 | tf_op jit(solution)/shard_map/ppermute | solution.py:40
  73.1 11.2 %collective-permute-done.11.refs_5_ = bf16[112,512]{1,0:T(8,128)(2,1)S(1)} collective-permute-done((bf16[112,512]{1,0:T(8,128)(2,1)S(1)}, bf16[112,512]{1,0:T(8,128)(2,1)S(1)}, u32[]{:S(2)}, u32[]{:S(2)}) %collective-permute-start.11) | collective-permute-done | bytes 114720 | tf_op jit(solution)/shard_map/ppermute | solution.py:40
  86.7 17.0 %shard_map.309 = (bf16[4,832,512]{2,1,0:T(8,128)(2,1)}, bf16[4,832,512]{2,1,0:T(8,128)(2,1)}, bf16[832,512]{1,0:T(8,128)(2,1)}, bf16[832,512]{1,0:T(8,128)(2,1)}...) custom-call(s32[6]{0:T(128)} %copy-done.9, bf16[832,512]{1,0:T(8,128)(2,1)} %bitcast.48, ...), custom_call_target="tpu_custom_call" | custom-call | tf_op jit(solution)/shard_map/pallas_call | solution.py:121
  103.7 5.8 %all-to-all-start.1 = ((bf16[8,104,512]{2,1,0:T(8,128)(2,1)}), bf16[8,104,512]{2,1,0:T(8,128)(2,1)S(1)}, u32[]{:S(2)}, u32[]{:S(2)}) async-start(bf16[8,104,512]{2,1,0:T(8,128)(2,1)} %bitcast.55), calls=%async_computation.1 | async-start | bytes 1703936 | tf_op jit(solution)/shard_map/all_to_all | solution.py:985
  109.5 4.9 %shard_map.310 = (bf16[704,512]{1,0:T(8,128)(2,1)}, bf16[336,512]{1,0:T(8,128)(2,1)}, f32[8,128]{1,0:T(8,128)}) custom-call(s32[6]{0:T(128)} %copy-done.9, bf16[832,512]{1,0:T(8,128)(2,1)} %bitcast.49, bf16[832,512]{1,0:T(8,128)(2,1)} %get-tuple-element.153.d_ref, bf16[4,832,512]{2,1,0:T(8,128)(2,1)} %get-tuple-element.151.hiddens, ...), custom_call_target="tpu_custom_call" | custom-call | tf_op jit(solution)/shard_map/pallas_call | solution.py:121
  115.9 10.5 %shard_map.311 = (bf16[880,512]{1,0:T(8,128)(2,1)}, bf16[160,512]{1,0:T(8,128)(2,1)}, bf16[1040,512]{1,0:T(8,128)(2,1)}, bf16[1040,512]{1,0:T(8,128)(2,1)}, f32[8,128]{1,0:T(8,128)}) custom-call(s32[6]{0:T(128)} %copy-done.9, bf16[832,512]{1,0:T(8,128)(2,1)} %bitcast.50, bf16[832,512]{1,0:T(8,128)(2,1)} %get-tuple-element.153.d_ref, ...), custom_call_target="tpu_custom_call" | custom-call | tf_op jit(solution)/shard_map/pallas_call | solution.py:121
  126.3 6.6 %collective-permute-done.15 = bf16[704,512]{1,0:T(8,128)(2,1)} collective-permute-done((bf16[704,512]{1,0:T(8,128)(2,1)}, bf16[704,512]{1,0:T(8,128)(2,1)}, u32[]{:S(2)}, u32[]{:S(2)}) %collective-permute-start.15) | collective-permute-done | bytes 720928 | tf_op jit(solution)/shard_map/ppermute | solution.py:40
  141.0 6.1 %collective-permute-done.18.rest_ref = bf16[208,512]{1,0:T(8,128)(2,1)S(1)} collective-permute-done((bf16[208,512]{1,0:T(8,128)(2,1)S(1)}, bf16[208,512]{1,0:T(8,128)(2,1)S(1)}, u32[]{:S(2)}, u32[]{:S(2)}) %collective-permute-start.18) | collective-permute-done | bytes 213024 | tf_op jit(solution)/shard_map/ppermute | solution.py:40
  147.0 3.8 %collective-permute-done.17.top_ref = bf16[208,512]{1,0:T(8,128)(2,1)S(1)} collective-permute-done((bf16[208,512]{1,0:T(8,128)(2,1)S(1)}, bf16[208,512]{1,0:T(8,128)(2,1)S(1)}, u32[]{:S(2)}, u32[]{:S(2)}) %collective-permute-start.17) | collective-permute-done | bytes 213024 | tf_op jit(solution)/shard_map/ppermute | solution.py:40
  152.3 8.5 %shard_map.313 = (bf16[416,512]{1,0:T(8,128)(2,1)}, f32[8,512]{1,0:T(8,128)}, bf16[416,512]{1,0:T(8,128)(2,1)}, f32[8,768]{1,0:T(8,128)}, bf16[2176,128]{1,0:T(8,128)(2,1)}, /*index=5*/bf16[2176,128]{1,0:T(8,128)(2,1)}) custom-call(s32[6]{0:T(128)} %copy-done.9, bf16[416,512]{1,0:T(8,128)(2,1)} %get-tuple-element.127.cot_ref, bf16[832,512]{1,0:T(8,128)(2,1)} %copy-done.5, ...), custom_call_target="tpu_custom_call" | custom-call | tf_op jit(solution)/shard_map/pallas_call | solution.py:121
  160.9 5.7 %all-to-all-start.2 = ((bf16[8,104,512]{2,1,0:T(8,128)(2,1)}), bf16[8,104,512]{2,1,0:T(8,128)(2,1)S(1)}, u32[]{:S(2)}, u32[]{:S(2)}) async-start(bf16[8,104,512]{2,1,0:T(8,128)(2,1)} %bitcast.16), calls=%async_computation.2 | async-start | bytes 1703936 | tf_op jit(solution)/shard_map/all_to_all | solution.py:985
  168.6 8.3 %shard_map.314 = (bf16[416,512]{1,0:T(8,128)(2,1)}, f32[8,512]{1,0:T(8,128)}, f32[8,768]{1,0:T(8,128)}, bf16[2176,128]{1,0:T(8,128)(2,1)}, bf16[2176,128]{1,0:T(8,128)(2,1)}) custom-call(s32[6]{0:T(128)} %copy-done.9, bf16[416,512]{1,0:T(8,128)(2,1)} %get-tuple-element.130.x_ref, bf16[416,512]{1,0:T(8,128)(2,1)} %get-tuple-element.176.d_normed_ref, ...), custom_call_target="tpu_custom_call" | custom-call | tf_op jit(solution)/shard_map/pallas_call | solution.py:121
  176.9 5.8 %collective-permute-done.21.far_ref = bf16[2176,128]{1,0:T(8,128)(2,1)S(1)} collective-permute-done((bf16[2176,128]{1,0:T(8,128)(2,1)S(1)}, bf16[2176,128]{1,0:T(8,128)(2,1)S(1)}, u32[]{:S(2)}, u32[]{:S(2)}) %collective-permute-start.21) | collective-permute-done | bytes 557088 | tf_op jit(solution)/shard_map/ppermute | solution.py:40
  188.9 4.3 %shard_map.316 = (bf16[832,512]{1,0:T(8,128)(2,1)S(1)}, bf16[832,512]{1,0:T(8,128)(2,1)}) custom-call(s32[6]{0:T(128)S(1)} %copy-done.12, s32[8,2,197]{2,1,0:T(2,128)S(1)} %bitcast.43, s32[8,2,197]{2,1,0:T(2,128)S(1)} %bitcast.47, bf16[832,512]{1,0:T(8,128)(2,1)S(1)} %bitcast.38), custom_call_target="tpu_custom_call" | custom-call | tf_op jit(solution)/shard_map/pallas_call | solution.py:121
  195.1 5.7 %all-to-all-start.3 = ((bf16[8,272,128]{2,1,0:T(8,128)(2,1)}), bf16[8,272,128]{2,1,0:T(8,128)(2,1)}, u32[]{:S(2)}, u32[]{:S(2)}) async-start(bf16[8,272,128]{2,1,0:T(8,128)(2,1)} %shard_map.315), calls=%async_computation.3 | async-start | bytes 1114112 | tf_op jit(solution)/shard_map/all_to_all | solution.py:1204
  208.9 3.6 %shard_map.318 = f32[1576,512]{1,0:T(8,128)} custom-call(s32[6]{0:T(128)S(1)} %copy-done.13, bf16[416,512]{1,0:T(8,128)(2,1)S(1)} %copy-done.8, bf16[416,512]{1,0:T(8,128)(2,1)S(1)} %collective-permute-done.24.refs_1_, bf16[416,512]{1,0:T(8,128)(2,1)S(1)} %collective-permute-done.25.refs_2_, bf16[416,512]{1,0:T(8,128)(2,1)S(1)} %collective-permute-done.26.refs_3_), custom_call_target="tpu_custom_call" | custom-call | tf_op jit(solution)/shard_map/pallas_call | solution.py:121
  220.9 5.9 %all-to-all-start.4 = ((bf16[8,368,128]{2,1,0:T(8,128)(2,1)}), bf16[8,368,128]{2,1,0:T(8,128)(2,1)S(1)}, u32[]{:S(2)}, u32[]{:S(2)}) async-start(bf16[8,368,128]{2,1,0:T(8,128)(2,1)} %shard_map.321), calls=%async_computation.4 | async-start | bytes 1507328 | tf_op jit(solution)/shard_map/all_to_all | solution.py:1265
  233.7 3.6 %shard_map.323 = f32[1576,512]{1,0:T(8,128)} custom-call(s32[6]{0:T(128)S(1)} %copy-done.14, bf16[832,512]{1,0:T(8,128)(2,1)S(1)} %get-tuple-element.210.refs_0_, bf16[832,512]{1,0:T(8,128)(2,1)S(1)} %collective-permute-done.32.refs_1_), custom_call_target="tpu_custom_call" | custom-call | tf_op jit(solution)/shard_map/pallas_call | solution.py:121
  240.9 3.6 %collective-permute-start.35 = (f32[8,128]{1,0:T(8,128)S(1)}, f32[8,128]{1,0:T(8,128)S(1)}, u32[]{:S(2)}, u32[]{:S(2)}) collective-permute-start(f32[8,128]{1,0:T(8,128)S(1)} %add.33), channel_id=1, source_target_pairs={{0,16},{4,20},{8,24},{12,28},{16,0},{20,4},{24,8},{28,12},{1,17},{... | collective-permute-start | bytes 12296 | tf_op jit(solution)/shard_map/ppermute | solution.py:40
  (197 shorter events, 92.3 us)
Async XLA Ops:
  2.4 15.5 %collective-permute-start.1 = (bf16[2080,128]{1,0:T(8,128)(2,1)S(1)}, bf16[2080,128]{1,0:T(8,128)(2,1)S(1)}, u32[]{:S(2)}, u32[]{:S(2)}) collective-permute-start(bf16[2080,128]{1,0:T(8,128)(2,1)S(1)} %shard_map.305.refs_3_.refs_7_.refs_0_), channel_id=1, source_target_pairs={{0,2},{1,3},{2,0},{3,1},{4,6},{5,7},{6,4},{7,5},{8,10},{9,11},{10,... | collective-permute-start | bytes 1597448 | tf_op jit(solution)/shard_map/ppermute | solution.py:40
  14.6 27.7 %collective-permute-start.8 = (bf16[1024,512]{1,0:T(8,128)(2,1)}, bf16[1024,512]{1,0:T(8,128)(2,1)}, u32[]{:S(2)}, u32[]{:S(2)}) collective-permute-start(bf16[1024,512]{1,0:T(8,128)(2,1)} %get-tuple-element.138), channel_id=1, source_target_pairs={{0,2},{1,3},{2,0},{3,1},{4,6},{5,7},{6,4},{7,5},{8,10},{9,11},{10,... | collective-permute-start | bytes 3145736 | tf_op jit(solution)/shard_map/ppermute | solution.py:40
  17.9 24.4 %collective-permute-start.5 = (bf16[448,512]{1,0:T(8,128)(2,1)}, bf16[448,512]{1,0:T(8,128)(2,1)S(1)}, u32[]{:S(2)}, u32[]{:S(2)}) collective-permute-start(bf16[448,512]{1,0:T(8,128)(2,1)} %get-tuple-element.133), channel_id=1, source_target_pairs={{0,16},{4,20},{8,24},{12,28},{16,0},{20,4},{24,8},{28,12},{1,17},{... | collective-permute-start | bytes 1376264 | tf_op jit(solution)/shard_map/ppermute | solution.py:40
  29.4 19.7 %collective-permute-start.4 = (bf16[416,512]{1,0:T(8,128)(2,1)S(1)}, bf16[416,512]{1,0:T(8,128)(2,1)S(1)}, u32[]{:S(2)}, u32[]{:S(2)}) collective-permute-start(bf16[416,512]{1,0:T(8,128)(2,1)S(1)} %get-tuple-element.132.refs_0_), channel_id=1, source_target_pairs={{0,2},{1,3},{2,0},{3,1},{4,6},{5,7},{6,4},{7,5},{8,10},{9,11},{10,... | collective-permute-start | bytes 1277960 | tf_op jit(solution)/shard_map/ppermute | solution.py:40
  31.5 10.9 %collective-permute-start.6 = (bf16[112,512]{1,0:T(8,128)(2,1)S(1)}, bf16[112,512]{1,0:T(8,128)(2,1)S(1)}, u32[]{:S(2)}, u32[]{:S(2)}) collective-permute-start(bf16[112,512]{1,0:T(8,128)(2,1)S(1)} %copy-done.45), channel_id=1, source_target_pairs={{0,4},{4,0},{8,12},{12,8},{16,20},{20,16},{24,28},{28,24},{1,5},{5... | collective-permute-start | bytes 344072 | tf_op jit(solution)/shard_map/ppermute | solution.py:40
  33.0 11.7 %collective-permute-start.7 = (bf16[112,512]{1,0:T(8,128)(2,1)S(1)}, bf16[112,512]{1,0:T(8,128)(2,1)S(1)}, u32[]{:S(2)}, u32[]{:S(2)}) collective-permute-start(bf16[112,512]{1,0:T(8,128)(2,1)S(1)} %copy-done.44), channel_id=1, source_target_pairs={{0,8},{4,12},{8,0},{12,4},{16,24},{20,28},{24,16},{28,20},{1,9},{5... | collective-permute-start | bytes 344072 | tf_op jit(solution)/shard_map/ppermute | solution.py:40
  54.4 31.4 %all-to-all-start = ((bf16[8,104,512]{2,1,0:T(8,128)(2,1)}), bf16[8,104,512]{2,1,0:T(8,128)(2,1)S(1)}, u32[]{:S(2)}, u32[]{:S(2)}) async-start(bf16[8,104,512]{2,1,0:T(8,128)(2,1)} %bitcast.11), calls=%async_computation | async-start | bytes 1703936 | tf_op jit(solution)/shard_map/all_to_all | solution.py:985
  60.5 23.8 %collective-permute-start.13 = (bf16[1024,512]{1,0:T(8,128)(2,1)}, bf16[1024,512]{1,0:T(8,128)(2,1)S(1)}, u32[]{:S(2)}, u32[]{:S(2)}) collective-permute-start(bf16[1024,512]{1,0:T(8,128)(2,1)} %get-tuple-element.148), channel_id=1, source_target_pairs={{0,1},{1,0},{2,3},{3,2},{4,5},{5,4},{6,7},{7,6},{8,9},{9,8},{10,11... | collective-permute-start | bytes 3145736 | tf_op jit(solution)/shard_map/ppermute | solution.py:40
  60.5 25.3 %collective-permute-start.14 = (bf16[1024,512]{1,0:T(8,128)(2,1)}, bf16[1024,512]{1,0:T(8,128)(2,1)}, u32[]{:S(2)}, u32[]{:S(2)}) collective-permute-start(bf16[1024,512]{1,0:T(8,128)(2,1)} %get-tuple-element.150), channel_id=1, source_target_pairs={{0,3},{1,2},{2,1},{3,0},{4,7},{5,6},{6,5},{7,4},{8,11},{9,10},{10,... | collective-permute-start | bytes 3145736 | tf_op jit(solution)/shard_map/ppermute | solution.py:40
  62.1 22.2 %collective-permute-start.12 = (bf16[224,512]{1,0:T(8,128)(2,1)S(1)}, bf16[224,512]{1,0:T(8,128)(2,1)S(1)}, u32[]{:S(2)}, u32[]{:S(2)}) collective-permute-start(bf16[224,512]{1,0:T(8,128)(2,1)S(1)} %get-tuple-element.146), channel_id=1, source_target_pairs={{0,12},{4,8},{8,4},{12,0},{16,28},{20,24},{24,20},{28,16},{1,13},{... | collective-permute-start | bytes 688136 | tf_op jit(solution)/shard_map/ppermute | solution.py:40
  65.6 18.7 %collective-permute-start.11 = (bf16[112,512]{1,0:T(8,128)(2,1)S(1)}, bf16[112,512]{1,0:T(8,128)(2,1)S(1)}, u32[]{:S(2)}, u32[]{:S(2)}) collective-permute-start(bf16[112,512]{1,0:T(8,128)(2,1)S(1)} %get-tuple-element.145), channel_id=1, source_target_pairs={{0,8},{4,12},{8,0},{12,4},{16,24},{20,28},{24,16},{28,20},{1,9},{5... | collective-permute-start | bytes 344072 | tf_op jit(solution)/shard_map/ppermute | solution.py:40
  103.7 29.3 %all-to-all-start.1 = ((bf16[8,104,512]{2,1,0:T(8,128)(2,1)}), bf16[8,104,512]{2,1,0:T(8,128)(2,1)S(1)}, u32[]{:S(2)}, u32[]{:S(2)}) async-start(bf16[8,104,512]{2,1,0:T(8,128)(2,1)} %bitcast.55), calls=%async_computation.1 | async-start | bytes 1703936 | tf_op jit(solution)/shard_map/all_to_all | solution.py:985
  114.4 18.5 %collective-permute-start.15 = (bf16[704,512]{1,0:T(8,128)(2,1)}, bf16[704,512]{1,0:T(8,128)(2,1)}, u32[]{:S(2)}, u32[]{:S(2)}) collective-permute-start(bf16[704,512]{1,0:T(8,128)(2,1)} %get-tuple-element.155), channel_id=1, source_target_pairs={{0,2},{1,3},{2,0},{3,1},{4,6},{5,7},{6,4},{7,5},{8,10},{9,11},{10,... | collective-permute-start | bytes 2162696 | tf_op jit(solution)/shard_map/ppermute | solution.py:40
  140.4 10.4 %collective-permute-start.17 = (bf16[208,512]{1,0:T(8,128)(2,1)S(1)}, bf16[208,512]{1,0:T(8,128)(2,1)S(1)}, u32[]{:S(2)}, u32[]{:S(2)}) collective-permute-start(bf16[208,512]{1,0:T(8,128)(2,1)S(1)} %get-tuple-element.236), channel_id=1, source_target_pairs={{0,2},{1,3},{2,0},{3,1},{4,6},{5,7},{6,4},{7,5},{8,10},{9,11},{10,... | collective-permute-start | bytes 638984 | tf_op jit(solution)/shard_map/ppermute | solution.py:40
  150.8 10.0 %collective-permute-start.19 = (bf16[336,512]{1,0:T(8,128)(2,1)S(1)}, bf16[336,512]{1,0:T(8,128)(2,1)S(1)}, u32[]{:S(2)}, u32[]{:S(2)}) collective-permute-start(bf16[336,512]{1,0:T(8,128)(2,1)S(1)} %copy-done.42), channel_id=1, source_target_pairs={{0,2},{1,3},{2,0},{3,1},{4,6},{5,7},{6,4},{7,5},{8,10},{9,11},{10,... | collective-permute-start | bytes 1032200 | tf_op jit(solution)/shard_map/ppermute | solution.py:40
  160.9 27.9 %all-to-all-start.2 = ((bf16[8,104,512]{2,1,0:T(8,128)(2,1)}), bf16[8,104,512]{2,1,0:T(8,128)(2,1)S(1)}, u32[]{:S(2)}, u32[]{:S(2)}) async-start(bf16[8,104,512]{2,1,0:T(8,128)(2,1)} %bitcast.16), calls=%async_computation.2 | async-start | bytes 1703936 | tf_op jit(solution)/shard_map/all_to_all | solution.py:985
  167.9 14.8 %collective-permute-start.21 = (bf16[2176,128]{1,0:T(8,128)(2,1)S(1)}, bf16[2176,128]{1,0:T(8,128)(2,1)S(1)}, u32[]{:S(2)}, u32[]{:S(2)}) collective-permute-start(bf16[2176,128]{1,0:T(8,128)(2,1)S(1)} %add_convert_fusion), channel_id=1, source_target_pairs={{0,2},{1,3},{2,0},{3,1},{4,6},{5,7},{6,4},{7,5},{8,10},{9,11},{10,... | collective-permute-start | bytes 1671176 | tf_op jit(solution)/shard_map/ppermute | solution.py:40
  182.7 12.4 %collective-permute-start.25 = (bf16[416,512]{1,0:T(8,128)(2,1)}, bf16[416,512]{1,0:T(8,128)(2,1)S(1)}, u32[]{:S(2)}, u32[]{:S(2)}) collective-permute-start(bf16[416,512]{1,0:T(8,128)(2,1)} %get-tuple-element.178.refs_0_), channel_id=1, source_target_pairs={{0,2},{1,3},{2,0},{3,1},{4,6},{5,7},{6,4},{7,5},{8,10},{9,11},{10,... | collective-permute-start | bytes 1277960 | tf_op jit(solution)/shard_map/ppermute | solution.py:40
  194.2 18.3 %collective-permute-start.27 = (bf16[1040,512]{1,0:T(8,128)(2,1)}, bf16[1040,512]{1,0:T(8,128)(2,1)S(1)}, u32[]{:S(2)}, u32[]{:S(2)}) collective-permute-start(bf16[1040,512]{1,0:T(8,128)(2,1)} %get-tuple-element.193), channel_id=1, source_target_pairs={{0,1},{1,0},{2,3},{3,2},{4,5},{5,4},{6,7},{7,6},{8,9},{9,8},{10,11... | collective-permute-start | bytes 3194888 | tf_op jit(solution)/shard_map/ppermute | solution.py:40
  195.1 22.7 %all-to-all-start.3 = ((bf16[8,272,128]{2,1,0:T(8,128)(2,1)}), bf16[8,272,128]{2,1,0:T(8,128)(2,1)}, u32[]{:S(2)}, u32[]{:S(2)}) async-start(bf16[8,272,128]{2,1,0:T(8,128)(2,1)} %shard_map.315), calls=%async_computation.3 | async-start | bytes 1114112 | tf_op jit(solution)/shard_map/all_to_all | solution.py:1204
  200.9 11.6 %collective-permute-start.28 = (bf16[704,512]{1,0:T(8,128)(2,1)}, bf16[704,512]{1,0:T(8,128)(2,1)S(1)}, u32[]{:S(2)}, u32[]{:S(2)}) collective-permute-start(bf16[704,512]{1,0:T(8,128)(2,1)} %collective-permute-done.15), channel_id=1, source_target_pairs={{0,1},{1,0},{2,3},{3,2},{4,5},{5,4},{6,7},{7,6},{8,9},{9,8},{10,11... | collective-permute-start | bytes 2162696 | tf_op jit(solution)/shard_map/ppermute | solution.py:40
  207.6 20.4 %collective-permute-start.31 = (bf16[832,512]{1,0:T(8,128)(2,1)}, bf16[832,512]{1,0:T(8,128)(2,1)S(1)}, u32[]{:S(2)}, u32[]{:S(2)}) collective-permute-start(bf16[832,512]{1,0:T(8,128)(2,1)} %shard_map.317.part_ref), channel_id=1, source_target_pairs={{0,2},{1,3},{2,0},{3,1},{4,6},{5,7},{6,4},{7,5},{8,10},{9,11},{10,... | collective-permute-start | bytes 2555912 | tf_op jit(solution)/shard_map/ppermute | solution.py:40
  220.9 26.2 %all-to-all-start.4 = ((bf16[8,368,128]{2,1,0:T(8,128)(2,1)}), bf16[8,368,128]{2,1,0:T(8,128)(2,1)S(1)}, u32[]{:S(2)}, u32[]{:S(2)}) async-start(bf16[8,368,128]{2,1,0:T(8,128)(2,1)} %shard_map.321), calls=%async_computation.4 | async-start | bytes 1507328 | tf_op jit(solution)/shard_map/all_to_all | solution.py:1265
  229.3 22.6 %collective-permute-start.36 = (bf16[880,512]{1,0:T(8,128)(2,1)}, bf16[880,512]{1,0:T(8,128)(2,1)S(1)}, u32[]{:S(2)}, u32[]{:S(2)}) collective-permute-start(bf16[880,512]{1,0:T(8,128)(2,1)} %get-tuple-element.217), channel_id=1, source_target_pairs={{0,2},{1,3},{2,0},{3,1},{4,6},{5,7},{6,4},{7,5},{8,10},{9,11},{10,... | collective-permute-start | bytes 2703368 | tf_op jit(solution)/shard_map/ppermute | solution.py:40
  (66 other events, 706.6 us)
